TPU v7x, 32 devices: a whole 2x2x4 slice. The times are simulated.
32 devices in a mesh: dp: 8 (over z, x), slab: 4 (over y, core).
Axes of the slice: x: 2, y: 2, z: 4, core: 2. Of those that a mesh axis runs over, the one named last changes fastest.
Arguments:
- inputs: bfloat16 [8, 24, 34944], P('dp', 'slab'), may hold values from -40 to 40
- upstream: bfloat16 [8, 24, 34944], P('dp', 'slab'), may hold values from -96 to 96
- labels: int32 [8, 24, 48], P('dp', 'slab'), may hold values from 0 to 2
- class_weights: float32 [3], replicated, may hold values from 0.25 to 4
- depth_kernel: bfloat16 [9, 728], replicated, may hold values from -2 to 2
- point_weight: bfloat16 [728, 728], replicated, may hold values from -0.21875 to 0.21875
- gain: float32 [728], replicated, may hold values from 0.5 to 1.5
- shift: float32 [728], replicated, may hold values from -3 to 3
Outputs:
- block_out: bfloat16 [8, 24, 34944], P('dp', 'slab')
- grad_input: bfloat16 [8, 24, 34944], P('dp', 'slab')
- grad_pointwise: float32 [728, 728], P(None, 'slab')
- grad_depthwise: float32 [9, 728], P(None, 'slab')
- grad_gain: float32 [728], P('slab')
- grad_shift: float32 [728], P('slab')
All inputs are finite; a program needn't handle non-finite values.
Results may differ from a plain program's by a relative error of at most 0.0052.
The roundings to bfloat16 on the way count: a program that leaves them out, or rounds other values in their place, can miss the bound.
Values may be sent and summed in bfloat16 or wider, within the bound.
No kernel may reach another device: no remote copies, remote signals or barrier semaphores. Data moves between devices by JAX's collectives and lax.ppermute only.
A program may use at most 64 MiB of HBM per device.

v0:
```python
import functools

import jax
import jax.numpy as jnp
from jax import lax
from jax.experimental import pallas as pl
from jax.experimental.pallas import tpu as pltpu
from jax.sharding import PartitionSpec as P

F32 = jnp.float32
BF16 = jnp.bfloat16
LANES = 128
SUB = 8
EPS = 1e-05
DMA = pltpu.SemaphoreType.DMA


def round_up(value, unit):
    return -(-value // unit) * unit


def tiles(width):
    return [(start, min(LANES, width - start)) for start in range(0, width, LANES)]


def column(ref, col, channels):
    start = col * channels
    base = start // LANES * LANES
    off = start - base
    end = min(ref.shape[1], base + round_up(off + channels, LANES))
    return ref[:, base:end].astype(F32)[:, off : off + channels]


def pixel_weights(class_ref, label_ref):
    labels = jnp.concatenate([label_ref[r] for r in range(label_ref.shape[0])], axis=0)
    weight = jnp.zeros(labels.shape, F32)
    for t in range(class_ref.shape[0]):
        weight = jnp.where(labels == t, class_ref[t], weight)
    return weight


def fetches(sources, buffers, sems):
    copies = [pltpu.make_async_copy(s, b, sems.at[i]) for i, (s, b) in enumerate(zip(sources, buffers))]
    for copy in copies:
        copy.start()
    return copies


def prepare_kernel(class_ref, x_ref, u_ref, label_ref, kernel_ref, active_ref, part_ref, grad_ref, class_buf, x_buf, u_buf, label_buf, kernel_buf, sems):
    rows, _, cols = label_buf.shape
    sub, channels = grad_ref.shape[1:]
    got_x, got_kernel, got_u, got_label, got_class = fetches(
        (x_ref.at[0], kernel_ref, u_ref.at[0], label_ref, class_ref), (x_buf, kernel_buf, u_buf, label_buf, class_buf), sems
    )
    got_x.wait()
    for col in range(cols):
        active_ref[col, :rows, :] = jnp.maximum(column(x_buf, col, channels), 0.0)
        active_ref[col, rows:, :] = jnp.zeros((sub - rows, channels), F32)
    got_kernel.wait()
    for start, width in tiles(channels):
        at = pl.ds(start, width)
        taps = [kernel_buf[t : t + 1, at].astype(F32) for t in range(9)]
        before = jnp.zeros((sub, width), F32)
        pending = before
        for col in range(cols):
            mid = active_ref[col, :, at]
            up = pltpu.roll(mid, 1, 0)
            down = pltpu.roll(mid, sub - 1, 0)
            sums = [taps[j] * up + taps[3 + j] * mid + taps[6 + j] * down for j in range(3)]
            if col:
                part_ref[col - 1, :, at] = pending + sums[2]
            pending = before + sums[1]
            before = sums[0]
        part_ref[cols - 1, :, at] = pending
    got_u.wait()
    got_label.wait()
    got_class.wait()
    weight = pixel_weights(class_buf, label_buf)
    for col in range(cols):
        grad_ref[col, :rows, :] = column(u_buf, col, channels) * weight[:, col : col + 1]
        grad_ref[col, rows:, :] = jnp.zeros((sub - rows, channels), F32)


def forward_kernel(pieces, rows, where_ref, part_ref, own_ref, one_ref, two_ref, kernel_ref, point_ref, grad_ref, depth_ref, proj_ref, active_ref, stats_ref, part_buf, active_buf, halo_buf, point_buf, kernel_buf, sems):
    cols, sub, channels = part_buf.shape
    got_kernel, got_point = fetches((kernel_ref, point_ref), (kernel_buf, point_buf), sems)
    put_active = pltpu.make_async_copy(active_buf, active_ref, sems.at[2])
    even = where_ref[0] % 2 == 0
    has_top = jnp.where(where_ref[0] > 0, 1.0, 0.0)
    has_bottom = jnp.where(where_ref[0] < pieces - 1, 1.0, 0.0)
    for col in range(cols):
        start = col * channels
        base = start // LANES * LANES
        off = start - base
        end = min(two_ref.shape[1], base + round_up(off + channels, LANES))
        near = one_ref[0, :, base:end].astype(F32)
        one = jnp.maximum(jnp.where(even, near[:1], near[rows - 1 :]), 0.0)
        two = jnp.maximum(two_ref[:, base:end].astype(F32), 0.0)
        top = jnp.where(even, two, one) * has_top
        bottom = jnp.where(even, one, two) * has_bottom
        line = lax.broadcasted_iota(jnp.int32, (sub, end - base), 0)
        lines = jnp.where(line == sub - 1, top, jnp.where(line == rows, bottom, 0.0))
        halo_buf[col] = lines[:, off : off + channels]
    got_kernel.wait()
    line = lax.broadcasted_iota(jnp.int32, (sub, channels), 0)
    wide = [
        jnp.where(line == sub - 1, kernel_buf[j : j + 1, :].astype(F32), kernel_buf[6 + j : 7 + j, :].astype(F32))
        for j in range(3)
    ]
    for start, width in tiles(channels):
        at = pl.ds(start, width)
        row = lax.broadcasted_iota(jnp.int32, (sub, width), 0)
        taps = [w[:, start : start + width] for w in wide]

        def finish(col, value):
            shifted = jnp.where(row == 0, pltpu.roll(value, 1, 0), jnp.where(row == rows - 1, pltpu.roll(value, sub - 1, 0), 0.0))
            total = part_ref[col, :, at] + shifted
            part_buf[col, :, at] = jnp.where(row < rows, total, 0.0)

        before = jnp.zeros((sub, width), F32)
        pending = before
        for col in range(cols):
            halo = halo_buf[col, :, at]
            active_buf[col, :, at] = own_ref[col, :, at] + halo
            if col:
                finish(col - 1, pending + taps[2] * halo)
            pending = before + taps[1] * halo
            before = taps[0] * halo
        finish(cols - 1, pending)
    put_active.start()
    depth = part_buf[...].reshape(cols * sub, channels).astype(BF16)
    depth_ref[:, :channels] = depth
    depth_ref[:, channels:] = jnp.zeros((cols * sub, depth_ref.shape[1] - channels), BF16)
    got_point.wait()
    proj_ref[...] = jnp.dot(depth, point_buf[...], preferred_element_type=F32)
    count = rows * cols
    for start, width in tiles(channels):
        at = pl.ds(start, width)
        proj = proj_ref[:, at]
        grads = grad_ref[:, :, at].reshape(cols * sub, width)
        mine = lax.broadcasted_iota(jnp.int32, (cols * sub, width), 0) % sub < rows
        center = jnp.sum(proj, axis=0, keepdims=True) / count
        deviation = jnp.where(mine, proj - center, 0.0)
        stats_ref[0:1, at] = center
        stats_ref[1:2, at] = jnp.sum(deviation * deviation, axis=0, keepdims=True)
        stats_ref[2:3, at] = jnp.sum(grads, axis=0, keepdims=True)
        stats_ref[3:4, at] = jnp.sum(grads * deviation, axis=0, keepdims=True)
        stats_ref[4:SUB, at] = jnp.zeros((SUB - 4, width), F32)
    put_active.wait()


def paired_sum(values):
    while len(values) > 1:
        values = [sum(values[i : i + 2]) for i in range(0, len(values), 2)]
    return values[0]


def cotangent_kernel(pieces, rows, proj_ref, grad_ref, gain_ref, _, *refs):
    stats_refs, (full_ref, norm_ref) = refs[:-2], refs[-2:]
    cols, sub, channels = grad_ref.shape
    local = rows * cols
    count = local * pieces
    stats = [ref[p : p + 4, :] for ref in stats_refs for p in range(0, ref.shape[0], SUB)]
    center = paired_sum([s[0:1] for s in stats]) / pieces
    square = paired_sum([s[1:2] + local * (s[0:1] - center) ** 2 for s in stats])
    shift_part = paired_sum([s[2:3] for s in stats])
    cross = paired_sum([s[3:4] + (s[0:1] - center) * s[2:3] for s in stats])
    inverse = lax.rsqrt(square / count + EPS)
    gain_part = cross * inverse
    gain = gain_ref[...].reshape(1, channels)
    norm_ref[0:1, :] = center
    norm_ref[1:2, :] = inverse
    norm_ref[2:3, :] = gain_part
    norm_ref[3:4, :] = shift_part
    norm_ref[4:SUB, :] = jnp.zeros((SUB - 4, channels), F32)
    for start, width in tiles(channels):
        at = slice(start, start + width)
        mine = lax.broadcasted_iota(jnp.int32, (cols * sub, width), 0) % sub < rows
        normed = (proj_ref[:, start : start + width] - center[:, at]) * inverse[:, at]
        grads = grad_ref[:, :, start : start + width].reshape(cols * sub, width)
        value = (gain * inverse)[:, at] * (grads - (shift_part / count)[:, at] - normed * (gain_part / count)[:, at])
        full_ref[:, start : start + width] = jnp.where(mine, value, 0.0).astype(BF16)
    full_ref[:, channels:] = jnp.zeros((cols * sub, full_ref.shape[1] - channels), BF16)


def product_kernel(full_ref, depth_ref, out_ref):
    channels = out_ref.shape[1]
    out_ref[...] = lax.dot_general(
        full_ref[:, :channels], depth_ref[:, :channels], (((0,), (0,)), ((), ())), preferred_element_type=F32
    )


def shares_kernel(pieces, share, where_ref, full_ref, depth_ref, own_ref, *refs):
    outs, total_ref = refs[:-1], refs[-1]
    product_kernel(full_ref, depth_ref, total_ref)
    for owner in range(pieces):

        @pl.when(where_ref[0] == owner)
        def _():
            def part(place):
                at = slice(place * share, (place + 1) * share)
                return total_ref[at, :] + own_ref[at, :]

            if pieces == 4:
                keep_ref, send_ref = outs
                keep_ref[...] = part(owner)
                send_ref[...] = part(owner ^ 2).astype(BF16)
            else:
                for j in range(pieces // 2):
                    outs[0][j] = part(2 * j + owner % 2)


def backward_kernel(rows, where_ref, full_ref, point_ref, active_ref, depth_grad_ref, tap_ref, one_ref, two_ref, point_buf, active_buf, grad_buf, sems):
    cols, sub, channels = active_buf.shape
    got_point, got_active = fetches((point_ref, active_ref), (point_buf, active_buf), sems)
    put = pltpu.make_async_copy(grad_buf, depth_grad_ref, sems.at[2])
    got_point.wait()
    grad = lax.dot_general(full_ref[:, :channels], point_buf[...], (((1,), (1,)), ((), ())), preferred_element_type=F32)
    grad_buf[...] = grad.astype(BF16).astype(F32).reshape(cols, sub, channels)
    put.start()
    even = where_ref[0] % 2 == 0
    first = grad_buf[:, 0, :].astype(BF16)
    last = grad_buf[:, rows - 1, :].astype(BF16)
    one_ref[...] = jnp.where(even, last, first)
    two_ref[...] = jnp.where(even, first, last)
    got_active.wait()
    for start, width in tiles(channels):
        at = pl.ds(start, width)
        totals = [jnp.zeros((sub, width), F32) for _ in range(9)]
        zero = jnp.zeros((sub, width), F32)
        ahead = grad_buf[0, :, at]
        here = zero
        for col in range(cols):
            behind, here = here, ahead
            ahead = grad_buf[col + 1, :, at] if col + 1 < cols else zero
            mid = active_buf[col, :, at]
            shifted = (pltpu.roll(mid, 1, 0), mid, pltpu.roll(mid, sub - 1, 0))
            for i in range(3):
                for j, other in enumerate((ahead, here, behind)):
                    totals[3 * i + j] = totals[3 * i + j] + shifted[i] * other
        for t in range(9):
            tap_ref[t : t + 1, at] = jnp.sum(totals[t], axis=0, keepdims=True)
        tap_ref[9:, at] = jnp.zeros((tap_ref.shape[0] - 9, width), F32)
    put.wait()


def fold(small, pieces, owner):
    share = small.shape[1] // pieces
    lines = -(-small.shape[0] // pieces)
    mine = small[:, owner * share : (owner + 1) * share]
    spare = lines * pieces - small.shape[0]
    if spare:
        mine = jnp.concatenate([mine, jnp.zeros((spare, share), F32)], axis=0)
    return jnp.concatenate([mine[q * lines : (q + 1) * lines] for q in range(pieces)], axis=1)


def unfold(lines, pieces, count):
    share = lines.shape[1] // pieces
    return jnp.concatenate([lines[:, q * share : (q + 1) * share] for q in range(pieces)], axis=0)[:count]


def store_halves(ref, start, lines):
    count = lines.shape[0]
    high = lines.astype(BF16).astype(F32)
    ref[start : start + count, :] = high
    ref[start + count : start + 2 * count, :] = lines - high


def small_kernel(pieces, where_ref, taps_ref, other_ref, norm_ref, stay_ref, leave_ref):
    taps = taps_ref[:9, :] + other_ref[:9, :]
    group = norm_ref[2:4, :]
    stay = jnp.concatenate([taps, group], axis=0)
    leave = jnp.concatenate([taps, jnp.zeros_like(group)], axis=0)
    for owner in range(pieces):

        @pl.when(where_ref[0] == owner)
        def _():
            stay_ref[...] = fold(stay, pieces, owner)
            leave_ref[...] = fold(leave, pieces, owner ^ 2)


def fold_kernel(pieces, where_ref, taps_ref, norm_ref, stay_ref, leave_ref):
    step = taps_ref.shape[0] // pieces
    taps = sum(taps_ref[p * step : p * step + 9, :] for p in range(pieces))
    small = jnp.concatenate([taps, norm_ref[2:4, :]], axis=0)
    for owner in range(pieces):

        @pl.when(where_ref[0] == owner)
        def _():
            stay_ref[...] = fold(small, pieces, owner)

    leave_ref[...] = jnp.zeros(leave_ref.shape, F32)


def pack_kernel(keep_ref, came_ref, fold_ref, other_ref, out_ref, flat_ref):
    copies, piece, channels = out_ref.shape
    share, lines = keep_ref.shape[0], fold_ref.shape[0]
    flat_ref[:share, :] = keep_ref[...] + came_ref[...].astype(F32)
    store_halves(flat_ref, share, fold_ref[...] + other_ref[...])
    rest = flat_ref.shape[0] - share - 2 * lines
    if rest:
        flat_ref[share + 2 * lines :, :] = jnp.zeros((rest, channels), F32)
    for k in range(copies):
        out_ref[k] = flat_ref[k * piece : (k + 1) * piece, :].astype(BF16)


def total_kernel(in_ref, out_ref):
    copies = in_ref.shape[0]
    total = in_ref[0].astype(F32)
    for k in range(1, copies):
        total = total + in_ref[k].astype(F32)
    total = total.astype(BF16)
    for k in range(copies):
        out_ref[k] = total


def unpack_kernel(pieces, batch, *refs):
    ins, (point_ref, tap_ref, gain_ref, shift_ref, flat_ref) = refs[:-5], refs[-5:]
    share = point_ref.shape[0]
    start = 0
    for in_ref in ins:
        copies, piece, _ = in_ref.shape
        for k in range(copies):
            flat_ref[start : start + piece, :] = in_ref[k].astype(F32) / batch
            start += piece
    point_ref[...] = flat_ref[:share, :]
    lines = -(-11 // pieces)
    total = flat_ref[share : share + lines, :] + flat_ref[share + lines : share + 2 * lines, :]
    small = unfold(total, pieces, 11)
    tap_ref[...] = small[:9]
    gain_ref[...] = small[9:10].reshape(share)
    shift_ref[...] = small[10:11].reshape(share)


def output_kernel(pieces, rows, where_ref, class_ref, x_ref, u_ref, label_ref, proj_ref, norm_ref, gain_ref, shift_ref, depth_grad_ref, one_ref, two_ref, kernel_ref, block_ref, input_ref, x_buf, u_buf, proj_buf, halo_buf, flat_ref, flat2_ref, class_buf, label_buf, kernel_buf, sems):
    cols, sub, channels = halo_buf.shape
    got_x, got_proj, got_grad, got_kernel, got_u, got_label, got_class = fetches(
        (x_ref.at[0], proj_ref, depth_grad_ref, kernel_ref, u_ref.at[0], label_ref, class_ref),
        (x_buf, proj_buf, halo_buf, kernel_buf, u_buf, label_buf, class_buf),
        sems,
    )
    even = where_ref[0] % 2 == 0
    has_top = jnp.where(where_ref[0] > 0, 1.0, 0.0)
    has_bottom = jnp.where(where_ref[0] < pieces - 1, 1.0, 0.0)
    center, inverse = norm_ref[0:1, :], norm_ref[1:2, :]
    gain, shift = gain_ref[...].reshape(1, channels), shift_ref[...].reshape(1, channels)
    got_x.wait()
    got_proj.wait()
    for col in range(cols):
        normed = (proj_buf[col * sub : col * sub + rows, :] - center) * inverse
        result = column(x_buf, col, channels) + gain * normed + shift
        flat_ref[:, col * channels : (col + 1) * channels] = result
    block_ref[...] = flat_ref[...].astype(BF16)
    one = one_ref[...].astype(F32)
    two = two_ref[...].astype(F32)
    top = jnp.where(even, two, one) * has_top
    bottom = jnp.where(even, one, two) * has_bottom
    line = lax.broadcasted_iota(jnp.int32, (sub, channels), 0)
    got_grad.wait()
    got_kernel.wait()
    for col in range(cols):
        halo_buf[col] = jnp.where(
            line == rows, bottom[col : col + 1], jnp.where(line == sub - 1, top[col : col + 1], halo_buf[col])
        )
    for start, width in tiles(channels):
        at = pl.ds(start, width)
        taps = [kernel_buf[t : t + 1, at].astype(F32) for t in range(9)]
        before = jnp.zeros((sub, width), F32)
        pending = before
        for col in range(cols):
            mid = halo_buf[col, :, at]
            up = pltpu.roll(mid, 1, 0)
            down = pltpu.roll(mid, sub - 1, 0)
            sums = [taps[j] * down + taps[3 + j] * mid + taps[6 + j] * up for j in range(3)]
            if col:
                halo_buf[col - 1, :, at] = pending + sums[0]
            pending = before + sums[1]
            before = sums[2]
        halo_buf[cols - 1, :, at] = pending
    got_u.wait()
    got_label.wait()
    got_class.wait()
    weight = pixel_weights(class_buf, label_buf)
    for col in range(cols):
        grads = column(u_buf, col, channels) * weight[:, col : col + 1]
        image = column(x_buf, col, channels)
        flat2_ref[:, col * channels : (col + 1) * channels] = grads + jnp.where(image > 0, halo_buf[col, :rows, :], 0.0)
    input_ref[...] = flat2_ref[...].astype(BF16)


def call(body, ins, outs, scratch=(), megabytes=16):
    space = {
        "o": pl.BlockSpec(memory_space=pl.ANY),
        "v": pl.BlockSpec(memory_space=pltpu.VMEM),
        "s": pl.BlockSpec(memory_space=pltpu.SMEM),
        "a": pl.BlockSpec(memory_space=pl.ANY),
    }
    return pl.pallas_call(
        body,
        out_shape=[jax.ShapeDtypeStruct(shape, dtype) for _, shape, dtype in outs],
        in_specs=[space[s] for s, _ in ins],
        out_specs=[space[s] for s, _, _ in outs],
        scratch_shapes=list(scratch),
        compiler_params=pltpu.CompilerParams(vmem_limit_bytes=megabytes * 1024 * 1024),
    )(*[pltpu.with_memory_space_constraint(a, pltpu.HBM) if s == "a" else a for s, a in ins])


def local(inputs, upstream, labels, class_weights, depth_kernel, point_weight, gain, shift):
    samples, rows, flat = inputs.shape
    assert samples == 1
    channels = point_weight.shape[0]
    cols = flat // channels
    pieces = lax.axis_size("slab")
    copies = lax.axis_size("dp")
    assert pieces % 2 == 0
    share = channels // pieces
    sub = round_up(rows + 2, SUB)
    padded = round_up(channels, LANES)
    me = lax.axis_index("slab")
    where = me.astype(jnp.int32).reshape(1)
    even = me % 2 == 0
    image = inputs.reshape(rows, flat)
    near = [(i, i ^ 1) for i in range(pieces)]
    far = [(i, (i - 1) % pieces if i % 2 == 0 else (i + 1) % pieces) for i in range(pieces)]
    lane3 = (cols, sub, channels)
    pixels = cols * sub
    buf3 = pltpu.VMEM(lane3, F32)
    flat_buf = pltpu.VMEM((rows, flat), BF16)
    flat_f32 = pltpu.VMEM((rows, flat), F32)
    point_buf = pltpu.VMEM((channels, channels), BF16)
    kernel_buf = pltpu.VMEM(depth_kernel.shape, BF16)
    label_buf = pltpu.VMEM((rows, 1, cols), labels.dtype)
    label_lines = jnp.transpose(labels, (1, 0, 2))
    class_buf = pltpu.SMEM(class_weights.shape, F32)

    one = lax.ppermute(inputs, "slab", near)
    two = lax.ppermute(lax.dynamic_slice_in_dim(image, jnp.where(even, 0, rows - 1), 1, 0), "slab", far)
    own, part, grad_out = call(
        prepare_kernel,
        [("a", class_weights), ("a", inputs), ("a", upstream), ("a", label_lines), ("a", depth_kernel)],
        [("v", lane3, F32), ("v", lane3, F32), ("v", lane3, F32)],
        [class_buf, flat_buf, flat_buf, label_buf, kernel_buf, DMA((5,))],
        megabytes=16,
    )
    depth, projected, active, stats = call(
        functools.partial(forward_kernel, pieces, rows),
        [("s", where), ("v", part), ("v", own), ("v", one), ("v", two), ("a", depth_kernel), ("a", point_weight), ("v", grad_out)],
        [("v", (pixels, padded), BF16), ("v", (pixels, channels), F32), ("a", lane3, F32), ("v", (SUB, channels), F32)],
        [buf3, buf3, buf3, point_buf, kernel_buf, DMA((3,))],
    )
    other_depth = lax.ppermute(depth, "slab", near)
    across = [(i, i ^ 2) for i in range(pieces)]
    if pieces == 4:
        apart = [(i, i ^ 3) for i in range(pieces)]
        all_stats = [stats, *(lax.ppermute(stats, "slab", pairs) for pairs in (near, across, apart))]
    else:
        all_stats = [lax.all_gather(stats, "slab", axis=0, tiled=True)]
    full, norm = call(
        functools.partial(cotangent_kernel, pieces, rows),
        [("v", projected), ("v", grad_out), ("v", gain), ("o", other_depth), *(("v", part) for part in all_stats)],
        [("v", (pixels, padded), BF16), ("v", (SUB, channels), F32)],
    )
    theirs = lax.ppermute(full, "slab", near)
    (own_product,) = call(product_kernel, [("v", full), ("v", depth)], [("v", (channels, channels), F32)])
    lines = -(-11 // pieces)
    batch = samples * copies
    if pieces == 4:
        share_outs = [("v", (share, channels), F32), ("v", (share, channels), BF16)]
    else:
        share_outs = [("v", (pieces // 2, share, channels), F32)]
    products = call(
        functools.partial(shares_kernel, pieces, share),
        [("s", where), ("v", theirs), ("v", other_depth), ("v", own_product)],
        share_outs,
        [pltpu.VMEM((channels, channels), F32)],
    )
    if pieces == 4:
        keep, leaving = products
    else:
        blocks = products[0]
        while blocks.shape[0] > 2:
            half = blocks.shape[0] // 2
            high = ((me // 2) & half) != 0
            mine = lax.dynamic_slice_in_dim(blocks, jnp.where(high, half, 0), half, 0)
            leaving = lax.dynamic_slice_in_dim(blocks, jnp.where(high, 0, half), half, 0).astype(BF16)
            came = lax.ppermute(leaving, "slab", [(i, i ^ (2 * half)) for i in range(pieces)])
            blocks = mine + came.astype(F32)
        bit = (me // 2) % 2
        keep = blocks[0] if pieces == 2 else lax.dynamic_index_in_dim(blocks, bit, 0, False)
        leaving = None if pieces == 2 else lax.dynamic_index_in_dim(blocks, 1 - bit, 0, False).astype(BF16)
    if pieces > 2:
        leaving, full = lax.optimization_barrier((leaving, full))
        came = lax.ppermute(leaving, "slab", across)
    else:
        came = jnp.zeros((share, channels), BF16)
    depth_grad, taps, edge_one, edge_two = call(
        functools.partial(backward_kernel, rows),
        [("s", where), ("v", full), ("o", point_weight), ("o", active)],
        [("a", lane3, F32), ("v", (2 * SUB, channels), F32), ("v", (cols, channels), BF16), ("v", (cols, channels), BF16)],
        [point_buf, buf3, buf3, DMA((3,))],
    )
    fold_outs = [("v", (lines, channels), F32)] * 2
    if pieces == 4:
        stay, leave = call(
            functools.partial(small_kernel, pieces),
            [("s", where), ("v", taps), ("v", lax.ppermute(taps, "slab", near)), ("v", norm)],
            fold_outs,
        )
        leave = lax.ppermute(leave, "slab", across)
    else:
        all_taps = lax.all_gather(taps, "slab", axis=0, tiled=True)
        stay, leave = call(functools.partial(fold_kernel, pieces), [("s", where), ("v", all_taps), ("v", norm)], fold_outs)
    piece = -(-(share + 2 * lines) // copies)
    total = piece * copies
    (packed,) = call(
        pack_kernel,
        [("v", keep), ("v", came), ("v", stay), ("v", leave)],
        [("v", (copies, piece, channels), BF16)],
        [pltpu.VMEM((total, channels), F32)],
    )
    landed = lax.all_to_all(packed, "dp", 0, 0)
    (summed,) = call(total_kernel, [("v", landed)], [("v", packed.shape, BF16)])
    gathered = lax.all_to_all(summed, "dp", 0, 0)
    halo_one = lax.ppermute(edge_one, "slab", near)
    halo_two = lax.ppermute(edge_two, "slab", far)
    block_out, grad_input = call(
        functools.partial(output_kernel, pieces, rows),
        [("s", where), ("a", class_weights), ("a", inputs), ("a", upstream), ("a", label_lines), ("a", projected), ("v", norm), ("v", gain), ("v", shift), ("a", depth_grad), ("v", halo_one), ("v", halo_two), ("a", depth_kernel)],
        [("v", (rows, flat), BF16), ("v", (rows, flat), BF16)],
        [flat_buf, flat_buf, pltpu.VMEM((pixels, channels), F32), buf3, flat_f32, flat_f32, class_buf, label_buf, kernel_buf, DMA((7,))],
        megabytes=16,
    )
    point_out, tap_out, gain_out, shift_out = call(
        functools.partial(unpack_kernel, pieces, batch),
        [("v", gathered)],
        [("v", (share, channels), F32), ("v", (9, share), F32), ("v", (share,), F32), ("v", (share,), F32)],
        [pltpu.VMEM((total, channels), F32)],
    )
    return (
        block_out.reshape(inputs.shape),
        grad_input.reshape(inputs.shape),
        point_out.T,
        tap_out,
        gain_out,
        shift_out,
    )


def solution(mesh):
    return jax.shard_map(
        local,
        mesh=mesh,
        in_specs=(
            P("dp", "slab", None),
            P("dp", "slab", None),
            P("dp", "slab", None),
            P(),
            P(),
            P(),
            P(),
            P(),
        ),
        out_specs=(
            P("dp", "slab", None),
            P("dp", "slab", None),
            P(None, "slab"),
            P(None, "slab"),
            P("slab"),
            P("slab"),
        ),
        check_vma=False,
    )
```

profile of v0, /device:TPU:0, one launch (start us, length us, event | category | flops | bytes accessed | tf_op | source)
XLA Modules:
  0.0 60.3 jit_solution(1672997528232143137)
XLA Ops:
  0.6 0.5 collective-permute-start
  1.1 1.2 %dynamic-slice_bitcast_fusion = bf16[1,34944]{1,0:T(2,128)(2,1)S(1)} fusion(bf16[1,6,34944]{2,1,0:T(8,128)(2,1)} %x_ref.3, s32[]{:T(128)S(6)} %select_n.13), kind=kLoop, calls=%fused_computation | loop fusion | bytes 139780 | tf_op jit(solution)/shard_map/dynamic_slice | solution.py:437
  2.4 2.7 %collective-permute-start.1 = (bf16[1,34944]{1,0:T(2,128)(2,1)S(1)}, bf16[1,34944]{1,0:T(2,128)(2,1)S(1)}, u32[]{:S(2)}, u32[]{:S(2)}) collective-permute-start(bf16[1,34944]{1,0:T(2,128)(2,1)S(1)} %dynamic-slice_bitcast_fusion), channel_id=1, source_target_pairs={{0,3},{1,2},{2,1},{3,0},{4,7},{5,6},{6,5},{7,4},{8,11},{9,10},{10,... | collective-permute-start | bytes 209672 | tf_op jit(solution)/shard_map/ppermute | solution.py:437
  5.0 4.7 %shard_map.127 = (f32[48,8,728]{2,1,0:T(8,128)S(1)}, f32[48,8,728]{2,1,0:T(8,128)S(1)}, f32[48,8,728]{2,1,0:T(8,128)S(1)}) custom-call(f32[3]{0:T(128)} %class_ref.3, bf16[1,6,34944]{2,1,0:T(8,128)(2,1)} %x_ref.3, bf16[1,6,34944]{2,1,0:T(8,128)(2,1)} %u_ref.3, s32[6,1,48]{2,1,0:T(1,128)} %bitcast.7, bf16[9,728]{1,0:T(8,128)(2,1)} %kernel_ref.5), custom_call_target="tpu_custom_call" | custom-call | tf_op jit(solution)/shard_map/pallas_call | solution.py:398
  9.8 3.0 %shard_map.128 = (bf16[384,768]{1,0:T(8,128)(2,1)S(1)}, f32[384,728]{1,0:T(8,128)S(1)}, f32[48,8,728]{2,1,0:T(8,128)S(1)}, f32[8,728]{1,0:T(8,128)S(1)}) custom-call(s32[1]{0:T(128)} %bitcast.where_ref, f32[48,8,728]{2,1,0:T(8,128)S(1)} %get-tuple-element.31.part_ref, f32[48,8,728]{2,1,0:T(8,128)S(1)} %get-tuple-element.32.own_ref, ...), custom_call_target="tpu_custom_call" | custom-call | tf_op jit(solution)/shard_map/pallas_call | solution.py:398
  12.8 0.1 collective-permute-start.2
  12.9 0.6 %collective-permute-start.5 = (f32[8,728]{1,0:T(8,128)S(1)}, f32[8,728]{1,0:T(8,128)S(1)}, u32[]{:S(2)}, u32[]{:S(2)}) collective-permute-start(f32[8,728]{1,0:T(8,128)S(1)} %get-tuple-element.36.refs_0_), channel_id=1, source_target_pairs={{0,3},{1,2},{2,1},{3,0},{4,7},{5,6},{6,5},{7,4},{8,11},{9,10},{10,... | collective-permute-start | bytes 69896 | tf_op jit(solution)/shard_map/ppermute | solution.py:455
  13.6 1.5 %collective-permute-start.4 = (f32[8,728]{1,0:T(8,128)S(1)}, f32[8,728]{1,0:T(8,128)S(1)}, u32[]{:S(2)}, u32[]{:S(2)}) collective-permute-start(f32[8,728]{1,0:T(8,128)S(1)} %get-tuple-element.36.refs_0_), channel_id=1, source_target_pairs={{0,2},{1,3},{2,0},{3,1},{4,6},{5,7},{6,4},{7,5},{8,10},{9,11},{10,... | collective-permute-start | bytes 69896 | tf_op jit(solution)/shard_map/ppermute | solution.py:455
  15.1 1.2 %collective-permute-done.5.refs_3_ = f32[8,728]{1,0:T(8,128)S(1)} collective-permute-done((f32[8,728]{1,0:T(8,128)S(1)}, f32[8,728]{1,0:T(8,128)S(1)}, u32[]{:S(2)}, u32[]{:S(2)}) %collective-permute-start.5) | collective-permute-done | bytes 23328 | tf_op jit(solution)/shard_map/ppermute | solution.py:455
  16.2 1.2 %collective-permute-done.4.refs_2_ = f32[8,728]{1,0:T(8,128)S(1)} collective-permute-done((f32[8,728]{1,0:T(8,128)S(1)}, f32[8,728]{1,0:T(8,128)S(1)}, u32[]{:S(2)}, u32[]{:S(2)}) %collective-permute-start.4) | collective-permute-done | bytes 23328 | tf_op jit(solution)/shard_map/ppermute | solution.py:455
  17.4 0.4 shard_map.129
  17.8 0.1 collective-permute-start.6
  17.9 0.8 %shard_map.130.own_ref = f32[728,728]{1,0:T(8,128)S(1)} custom-call(bf16[384,768]{1,0:T(8,128)(2,1)S(1)} %get-tuple-element.40.full_ref, bf16[384,768]{1,0:T(8,128)(2,1)S(1)} %get-tuple-element.35.depth_ref), custom_call_target="tpu_custom_call" | custom-call | tf_op jit(solution)/shard_map/pallas_call | solution.py:398
  18.7 1.2 %collective-permute-done.6.full_ref = bf16[384,768]{1,0:T(8,128)(2,1)S(1)} collective-permute-done((bf16[384,768]{1,0:T(8,128)(2,1)S(1)}, bf16[384,768]{1,0:T(8,128)(2,1)S(1)}, u32[]{:S(2)}, u32[]{:S(2)}) %collective-permute-start.6) | collective-permute-done | bytes 589856 | tf_op jit(solution)/shard_map/ppermute | solution.py:463
  19.9 1.0 %shard_map.131 = (f32[182,728]{1,0:T(8,128)S(1)}, bf16[182,728]{1,0:T(8,128)(2,1)S(1)}) custom-call(s32[1]{0:T(128)} %bitcast.where_ref, bf16[384,768]{1,0:T(8,128)(2,1)S(1)} %collective-permute-done.6.full_ref, bf16[384,768]{1,0:T(8,128)(2,1)S(1)} %collective-permute-done.2._.depth_ref, f32[728,728]{1,0:T(8,128)S(1)} %shard_map.130.own_ref), custom_call_target="tpu_custom_call" | custom-call | tf_op jit(solution)/shard_map/pallas_call | solution.py:398
  20.9 1.6 %collective-permute-start.9 = (bf16[182,728]{1,0:T(8,128)(2,1)S(1)}, bf16[182,728]{1,0:T(8,128)(2,1)S(1)}, u32[]{:S(2)}, u32[]{:S(2)}) collective-permute-start(bf16[182,728]{1,0:T(8,128)(2,1)S(1)} %get-tuple-element.48), channel_id=1, source_target_pairs={{0,2},{1,3},{2,0},{3,1},{4,6},{5,7},{6,4},{7,5},{8,10},{9,11},{10,... | collective-permute-start | bytes 794984 | tf_op jit(solution)/shard_map/ppermute | solution.py:493
  22.5 2.7 %shard_map.132 = (f32[48,8,728]{2,1,0:T(8,128)S(1)}, f32[16,728]{1,0:T(8,128)S(1)}, bf16[48,728]{1,0:T(8,128)(2,1)S(1)}, bf16[48,728]{1,0:T(8,128)(2,1)S(1)}) custom-call(s32[1]{0:T(128)} %bitcast.where_ref, bf16[384,768]{1,0:T(8,128)(2,1)S(1)} %get-tuple-element.40.full_ref, bf16[728,728]{1,0:T(8,128)(2,1)S(1)} %copy-done.1, ...), custom_call_target="tpu_custom_call" | custom-call | tf_op jit(solution)/shard_map/pallas_call | solution.py:398
  25.2 1.0 %copy-done.2 = f32[48,8,728]{2,1,0:T(8,128)} copy-done((f32[48,8,728]{2,1,0:T(8,128)}, f32[48,8,728]{2,1,0:T(8,128)S(1)}, u32[]{:S(2)}) %copy-start.2) | copy-done | bytes 1118232
  26.2 1.2 %collective-permute-done.10.other_ref = f32[16,728]{1,0:T(8,128)S(1)} collective-permute-done((f32[16,728]{1,0:T(8,128)S(1)}, f32[16,728]{1,0:T(8,128)S(1)}, u32[]{:S(2)}, u32[]{:S(2)}) %collective-permute-start.10) | collective-permute-done | bytes 46624 | tf_op jit(solution)/shard_map/ppermute | solution.py:506
  27.5 0.1 shard_map.134
  27.6 0.6 collective-permute-start.11
  28.1 3.2 %collective-permute-done.11.other_ref = f32[3,728]{1,0:T(4,128)S(1)} collective-permute-done((f32[3,728]{1,0:T(4,128)S(1)}, f32[3,728]{1,0:T(4,128)S(1)}, u32[]{:S(2)}, u32[]{:S(2)}) %collective-permute-start.11) | collective-permute-done | bytes 8768 | tf_op jit(solution)/shard_map/ppermute | solution.py:509
  31.4 0.1 shard_map.135
  31.5 15.1 %all_to_all.10.in_ref = bf16[8,24,728]{2,1,0:T(8,128)(2,1)S(1)} all-to-all(bf16[8,24,728]{2,1,0:T(8,128)(2,1)S(1)} %shard_map.135), channel_id=1, replica_groups=mesh['dp'=8,'slab'=4] {'dp'}, dimensions={0} | all-to-all | bytes 559104 | tf_op jit(solution)/shard_map/all_to_all | solution.py:521
  46.6 0.8 %shard_map.136 = bf16[8,24,728]{2,1,0:T(8,128)(2,1)} custom-call(bf16[8,24,728]{2,1,0:T(8,128)(2,1)S(1)} %all_to_all.10.in_ref), custom_call_target="tpu_custom_call" | custom-call | tf_op jit(solution)/shard_map/pallas_call | solution.py:398
  47.3 3.4 %all-to-all-start.1 = ((bf16[8,24,728]{2,1,0:T(8,128)(2,1)}), bf16[8,24,728]{2,1,0:T(8,128)(2,1)S(1)}, u32[]{:S(2)}, u32[]{:S(2)}) async-start(bf16[8,24,728]{2,1,0:T(8,128)(2,1)} %shard_map.136), calls=%async_computation.1 | async-start | bytes 589824 | tf_op jit(solution)/shard_map/all_to_all | solution.py:523
  50.8 0.1 collective-permute-start.7
  50.8 1.1 %collective-permute-start.8 = (bf16[48,728]{1,0:T(8,128)(2,1)S(1)}, bf16[48,728]{1,0:T(8,128)(2,1)S(1)}, u32[]{:S(2)}, u32[]{:S(2)}) collective-permute-start(bf16[48,728]{1,0:T(8,128)(2,1)S(1)} %get-tuple-element.44), channel_id=1, source_target_pairs={{0,3},{1,2},{2,1},{3,0},{4,7},{5,6},{6,5},{7,4},{8,11},{9,10},{10,... | collective-permute-start | bytes 209672 | tf_op jit(solution)/shard_map/ppermute | solution.py:525
  52.0 0.1 collective-permute-done.7.one_ref
  52.1 2.8 %collective-permute-done.8.two_ref = bf16[48,728]{1,0:T(8,128)(2,1)S(1)} collective-permute-done((bf16[48,728]{1,0:T(8,128)(2,1)S(1)}, bf16[48,728]{1,0:T(8,128)(2,1)S(1)}, u32[]{:S(2)}, u32[]{:S(2)}) %collective-permute-start.8) | collective-permute-done | bytes 69920 | tf_op jit(solution)/shard_map/ppermute | solution.py:525
  54.9 4.5 %shard_map.133 = (bf16[6,34944]{1,0:T(8,128)(2,1)}, bf16[6,34944]{1,0:T(8,128)(2,1)}) custom-call(s32[1]{0:T(128)} %bitcast.where_ref, f32[3]{0:T(128)} %class_ref.3, bf16[1,6,34944]{2,1,0:T(8,128)(2,1)} %x_ref.3, bf16[1,6,34944]{2,1,0:T(8,128)(2,1)} %u_ref.3, s32[6,1,48]{2,1,0:T(1,128)} %bitcast.8, f32[384,728]{1,0:T(8,128)} %copy-done, ...), custom_call_target="tpu_custom_call" | custom-call | tf_op jit(solution)/shard_map/pallas_call | solution.py:398
  59.4 0.9 %shard_map.137 = (f32[182,728]{1,0:T(8,128)}, f32[9,182]{1,0:T(8,128)}, f32[182]{0:T(256)}, f32[182]{0:T(256)}) custom-call(bf16[8,24,728]{2,1,0:T(8,128)(2,1)S(1)} %all-to-all-done.1.refs_0_), custom_call_target="tpu_custom_call" | custom-call | tf_op jit(solution)/shard_map/pallas_call | solution.py:398
  (17 shorter events, 0.0 us)
Async XLA Ops:
  0.6 9.2 %collective-permute-start = (bf16[1,6,34944]{2,1,0:T(8,128)(2,1)}, bf16[1,6,34944]{2,1,0:T(8,128)(2,1)S(1)}, u32[]{:S(2)}, u32[]{:S(2)}) collective-permute-start(bf16[1,6,34944]{2,1,0:T(8,128)(2,1)} %x_ref.3), channel_id=1, source_target_pairs={{0,1},{1,0},{2,3},{3,2},{4,5},{5,4},{6,7},{7,6},{8,9},{9,8},{10,11... | collective-permute-start | bytes 1257992 | tf_op jit(solution)/shard_map/ppermute | solution.py:436
  2.4 7.4 %collective-permute-start.1 = (bf16[1,34944]{1,0:T(2,128)(2,1)S(1)}, bf16[1,34944]{1,0:T(2,128)(2,1)S(1)}, u32[]{:S(2)}, u32[]{:S(2)}) collective-permute-start(bf16[1,34944]{1,0:T(2,128)(2,1)S(1)} %dynamic-slice_bitcast_fusion), channel_id=1, source_target_pairs={{0,3},{1,2},{2,1},{3,0},{4,7},{5,6},{6,5},{7,4},{8,11},{9,10},{10,... | collective-permute-start | bytes 209672 | tf_op jit(solution)/shard_map/ppermute | solution.py:437
  9.8 7.6 %copy-start.3 = (f32[728]{0:T(1024)S(1)}, f32[728]{0:T(1024)}, u32[]{:S(2)}) copy-start(f32[728]{0:T(1024)} %gain_ref.3) | copy-start | bytes 8740
  12.8 5.0 %copy-start = (f32[384,728]{1,0:T(8,128)}, f32[384,728]{1,0:T(8,128)S(1)}, u32[]{:S(2)}) copy-start(f32[384,728]{1,0:T(8,128)S(1)} %get-tuple-element.34.proj_ref) | copy-start | bytes 3354628
  12.8 4.6 %collective-permute-start.2 = (bf16[384,768]{1,0:T(8,128)(2,1)S(1)}, bf16[384,768]{1,0:T(8,128)(2,1)S(1)}, u32[]{:S(2)}, u32[]{:S(2)}) collective-permute-start(bf16[384,768]{1,0:T(8,128)(2,1)S(1)} %get-tuple-element.35.depth_ref), channel_id=1, source_target_pairs={{0,1},{1,0},{2,3},{3,2},{4,5},{5,4},{6,7},{7,6},{8,9},{9,8},{10,11... | collective-permute-start | bytes 1769480 | tf_op jit(solution)/shard_map/ppermute | solution.py:451
  12.9 3.3 %collective-permute-start.5 = (f32[8,728]{1,0:T(8,128)S(1)}, f32[8,728]{1,0:T(8,128)S(1)}, u32[]{:S(2)}, u32[]{:S(2)}) collective-permute-start(f32[8,728]{1,0:T(8,128)S(1)} %get-tuple-element.36.refs_0_), channel_id=1, source_target_pairs={{0,3},{1,2},{2,1},{3,0},{4,7},{5,6},{6,5},{7,4},{8,11},{9,10},{10,... | collective-permute-start | bytes 69896 | tf_op jit(solution)/shard_map/ppermute | solution.py:455
  13.6 3.8 %collective-permute-start.4 = (f32[8,728]{1,0:T(8,128)S(1)}, f32[8,728]{1,0:T(8,128)S(1)}, u32[]{:S(2)}, u32[]{:S(2)}) collective-permute-start(f32[8,728]{1,0:T(8,128)S(1)} %get-tuple-element.36.refs_0_), channel_id=1, source_target_pairs={{0,2},{1,3},{2,0},{3,1},{4,6},{5,7},{6,4},{7,5},{8,10},{9,11},{10,... | collective-permute-start | bytes 69896 | tf_op jit(solution)/shard_map/ppermute | solution.py:455
  15.1 2.3 %collective-permute-start.3 = (f32[8,728]{1,0:T(8,128)S(1)}, f32[8,728]{1,0:T(8,128)S(1)}, u32[]{:S(2)}, u32[]{:S(2)}) collective-permute-start(f32[8,728]{1,0:T(8,128)S(1)} %get-tuple-element.36.refs_0_), channel_id=1, source_target_pairs={{0,1},{1,0},{2,3},{3,2},{4,5},{5,4},{6,7},{7,6},{8,9},{9,8},{10,11... | collective-permute-start | bytes 69896 | tf_op jit(solution)/shard_map/ppermute | solution.py:455
  17.8 2.1 %collective-permute-start.6 = (bf16[384,768]{1,0:T(8,128)(2,1)S(1)}, bf16[384,768]{1,0:T(8,128)(2,1)S(1)}, u32[]{:S(2)}, u32[]{:S(2)}) collective-permute-start(bf16[384,768]{1,0:T(8,128)(2,1)S(1)} %get-tuple-element.40.full_ref), channel_id=1, source_target_pairs={{0,1},{1,0},{2,3},{3,2},{4,5},{5,4},{6,7},{7,6},{8,9},{9,8},{10,11... | collective-permute-start | bytes 1769480 | tf_op jit(solution)/shard_map/ppermute | solution.py:463
  18.7 3.8 %copy-start.1 = (bf16[728,728]{1,0:T(8,128)(2,1)S(1)}, bf16[728,728]{1,0:T(8,128)(2,1)}, u32[]{:S(2)}) copy-start(bf16[728,728]{1,0:T(8,128)(2,1)} %point_ref.3) | copy-start | bytes 3179908
  20.9 10.5 %collective-permute-start.9 = (bf16[182,728]{1,0:T(8,128)(2,1)S(1)}, bf16[182,728]{1,0:T(8,128)(2,1)S(1)}, u32[]{:S(2)}, u32[]{:S(2)}) collective-permute-start(bf16[182,728]{1,0:T(8,128)(2,1)S(1)} %get-tuple-element.48), channel_id=1, source_target_pairs={{0,2},{1,3},{2,0},{3,1},{4,6},{5,7},{6,4},{7,5},{8,10},{9,11},{10,... | collective-permute-start | bytes 794984 | tf_op jit(solution)/shard_map/ppermute | solution.py:493
  25.2 1.0 %copy-start.2 = (f32[48,8,728]{2,1,0:T(8,128)}, f32[48,8,728]{2,1,0:T(8,128)S(1)}, u32[]{:S(2)}) copy-start(f32[48,8,728]{2,1,0:T(8,128)S(1)} %get-tuple-element.42.depth_grad_ref) | copy-start | bytes 3354628
  26.2 1.2 %collective-permute-start.10 = (f32[16,728]{1,0:T(8,128)S(1)}, f32[16,728]{1,0:T(8,128)S(1)}, u32[]{:S(2)}, u32[]{:S(2)}) collective-permute-start(f32[16,728]{1,0:T(8,128)S(1)} %get-tuple-element.49.taps_ref), channel_id=1, source_target_pairs={{0,1},{1,0},{2,3},{3,2},{4,5},{5,4},{6,7},{7,6},{8,9},{9,8},{10,11... | collective-permute-start | bytes 139784 | tf_op jit(solution)/shard_map/ppermute | solution.py:506
  27.6 3.8 %collective-permute-start.11 = (f32[3,728]{1,0:T(4,128)S(1)}, f32[3,728]{1,0:T(4,128)S(1)}, u32[]{:S(2)}, u32[]{:S(2)}) collective-permute-start(f32[3,728]{1,0:T(4,128)S(1)} %get-tuple-element.51), channel_id=1, source_target_pairs={{0,2},{1,3},{2,0},{3,1},{4,6},{5,7},{6,4},{7,5},{8,10},{9,11},{10,... | collective-permute-start | bytes 26216 | tf_op jit(solution)/shard_map/ppermute | solution.py:509
  31.4 23.5 %copy-start.4 = (f32[728]{0:T(1024)S(1)}, f32[728]{0:T(1024)}, u32[]{:S(2)}) copy-start(f32[728]{0:T(1024)} %shift_ref.1) | copy-start | bytes 8740
  47.3 12.1 %all-to-all-start.1 = ((bf16[8,24,728]{2,1,0:T(8,128)(2,1)}), bf16[8,24,728]{2,1,0:T(8,128)(2,1)S(1)}, u32[]{:S(2)}, u32[]{:S(2)}) async-start(bf16[8,24,728]{2,1,0:T(8,128)(2,1)} %shard_map.136), calls=%async_computation.1 | async-start | bytes 589824 | tf_op jit(solution)/shard_map/all_to_all | solution.py:523
  50.8 1.3 %collective-permute-start.7 = (bf16[48,728]{1,0:T(8,128)(2,1)S(1)}, bf16[48,728]{1,0:T(8,128)(2,1)S(1)}, u32[]{:S(2)}, u32[]{:S(2)}) collective-permute-start(bf16[48,728]{1,0:T(8,128)(2,1)S(1)} %get-tuple-element.43), channel_id=1, source_target_pairs={{0,1},{1,0},{2,3},{3,2},{4,5},{5,4},{6,7},{7,6},{8,9},{9,8},{10,11... | collective-permute-start | bytes 209672 | tf_op jit(solution)/shard_map/ppermute | solution.py:524
  50.8 4.1 %collective-permute-start.8 = (bf16[48,728]{1,0:T(8,128)(2,1)S(1)}, bf16[48,728]{1,0:T(8,128)(2,1)S(1)}, u32[]{:S(2)}, u32[]{:S(2)}) collective-permute-start(bf16[48,728]{1,0:T(8,128)(2,1)S(1)} %get-tuple-element.44), channel_id=1, source_target_pairs={{0,3},{1,2},{2,1},{3,0},{4,7},{5,6},{6,5},{7,4},{8,11},{9,10},{10,... | collective-permute-start | bytes 209672 | tf_op jit(solution)/shard_map/ppermute | solution.py:525
where the time goes:
time: 60.6 us; the launch traced here: 60.3 us
  Pallas kernels  19 us (31%)
  blocking collectives  15.1 us (25%)
  starting transfers between devices  12.3 us (20%)
  waiting for transfers between devices  10.9 us (18%)
  local copies, waits for them, and re-layouts  2.24 us (4%)
  between operations  0.8 us (1%)
    pallas_call x11, Pallas kernels, call(): pl.pallas_call(body, out_shape=[jax.ShapeDtypeStruct(shape, dtype) for _,...  19 us
    all_to_all x1, blocking collectives, local(): landed = lax.all_to_all(packed, 'dp', 0, 0)  15.1 us
    all_to_all x1, starting transfers between devices, local(): gathered = lax.all_to_all(summed, 'dp', 0, 0)  3.42 us
    ppermute x1, waiting for transfers between devices, local(): leave = lax.ppermute(leave, 'slab', across)  3.21 us
    ppermute x1, waiting for transfers between devices, local(): halo_two = lax.ppermute(edge_two, 'slab', far)  2.81 us
    ppermute x1, starting transfers between devices, local(): lax.ppermute(lax.dynamic_slice_in_dim(image, jnp.where(even, 0, rows - 1)...  2.69 us
    ppermute x3, waiting for transfers between devices, local(): lax.ppermute(stats, 'slab', pairs)  2.33 us
    ppermute x3, starting transfers between devices, local(): lax.ppermute(stats, 'slab', pairs)  2.12 us
  transfers between devices with their start and end apart: 13, of which 7 were waited for; matrix products, arithmetic and copies ran while one was open for 2% of the time, Pallas kernels for 21%

commit v1 on v0

--- a/solution.py
+++ b/solution.py
@@ -52,10 +52,10 @@
     got_x, got_kernel, got_u, got_label, got_class = fetches(
         (x_ref.at[0], kernel_ref, u_ref.at[0], label_ref, class_ref), (x_buf, kernel_buf, u_buf, label_buf, class_buf), sems
     )
+    below = jnp.zeros((sub - rows, channels), F32)
     got_x.wait()
     for col in range(cols):
-        active_ref[col, :rows, :] = jnp.maximum(column(x_buf, col, channels), 0.0)
-        active_ref[col, rows:, :] = jnp.zeros((sub - rows, channels), F32)
+        active_ref[col] = jnp.concatenate([jnp.maximum(column(x_buf, col, channels), 0.0), below], axis=0)
     got_kernel.wait()
     for start, width in tiles(channels):
         at = pl.ds(start, width)
@@ -77,8 +77,7 @@
     got_class.wait()
     weight = pixel_weights(class_buf, label_buf)
     for col in range(cols):
-        grad_ref[col, :rows, :] = column(u_buf, col, channels) * weight[:, col : col + 1]
-        grad_ref[col, rows:, :] = jnp.zeros((sub - rows, channels), F32)
+        grad_ref[col] = jnp.concatenate([column(u_buf, col, channels) * weight[:, col : col + 1], below], axis=0)
 
 
 def forward_kernel(pieces, rows, where_ref, part_ref, own_ref, one_ref, two_ref, kernel_ref, point_ref, grad_ref, depth_ref, proj_ref, active_ref, stats_ref, part_buf, active_buf, halo_buf, point_buf, kernel_buf, sems):
@@ -86,20 +85,19 @@
     got_kernel, got_point = fetches((kernel_ref, point_ref), (kernel_buf, point_buf), sems)
     put_active = pltpu.make_async_copy(active_buf, active_ref, sems.at[2])
     even = where_ref[0] % 2 == 0
-    has_top = jnp.where(where_ref[0] > 0, 1.0, 0.0)
-    has_bottom = jnp.where(where_ref[0] < pieces - 1, 1.0, 0.0)
+    near_line = jnp.where(even, rows, sub - 1)
+    far_line = jnp.where(even, sub - 1, rows)
+    far_line = jnp.where((where_ref[0] == 0) | (where_ref[0] == pieces - 1), sub, far_line)
     for col in range(cols):
         start = col * channels
         base = start // LANES * LANES
         off = start - base
         end = min(two_ref.shape[1], base + round_up(off + channels, LANES))
         near = one_ref[0, :, base:end].astype(F32)
-        one = jnp.maximum(jnp.where(even, near[:1], near[rows - 1 :]), 0.0)
-        two = jnp.maximum(two_ref[:, base:end].astype(F32), 0.0)
-        top = jnp.where(even, two, one) * has_top
-        bottom = jnp.where(even, one, two) * has_bottom
+        one = jnp.where(even, near[:1], near[rows - 1 :])
+        two = two_ref[:, base:end].astype(F32)
         line = lax.broadcasted_iota(jnp.int32, (sub, end - base), 0)
-        lines = jnp.where(line == sub - 1, top, jnp.where(line == rows, bottom, 0.0))
+        lines = jnp.maximum(jnp.where(line == near_line, one, jnp.where(line == far_line, two, 0.0)), 0.0)
         halo_buf[col] = lines[:, off : off + channels]
     got_kernel.wait()
     line = lax.broadcasted_iota(jnp.int32, (sub, channels), 0)
@@ -332,16 +330,11 @@
     shift_ref[...] = small[10:11].reshape(share)
 
 
-def output_kernel(pieces, rows, where_ref, class_ref, x_ref, u_ref, label_ref, proj_ref, norm_ref, gain_ref, shift_ref, depth_grad_ref, one_ref, two_ref, kernel_ref, block_ref, input_ref, x_buf, u_buf, proj_buf, halo_buf, flat_ref, flat2_ref, class_buf, label_buf, kernel_buf, sems):
-    cols, sub, channels = halo_buf.shape
-    got_x, got_proj, got_grad, got_kernel, got_u, got_label, got_class = fetches(
-        (x_ref.at[0], proj_ref, depth_grad_ref, kernel_ref, u_ref.at[0], label_ref, class_ref),
-        (x_buf, proj_buf, halo_buf, kernel_buf, u_buf, label_buf, class_buf),
-        sems,
-    )
-    even = where_ref[0] % 2 == 0
-    has_top = jnp.where(where_ref[0] > 0, 1.0, 0.0)
-    has_bottom = jnp.where(where_ref[0] < pieces - 1, 1.0, 0.0)
+def block_kernel(rows, x_ref, proj_ref, norm_ref, gain_ref, shift_ref, block_ref, x_buf, proj_buf, flat_ref, sems):
+    channels = proj_buf.shape[1]
+    cols = flat_ref.shape[1] // channels
+    sub = proj_buf.shape[0] // cols
+    got_x, got_proj = fetches((x_ref.at[0], proj_ref), (x_buf, proj_buf), sems)
     center, inverse = norm_ref[0:1, :], norm_ref[1:2, :]
     gain, shift = gain_ref[...].reshape(1, channels), shift_ref[...].reshape(1, channels)
     got_x.wait()
@@ -351,6 +344,18 @@
         result = column(x_buf, col, channels) + gain * normed + shift
         flat_ref[:, col * channels : (col + 1) * channels] = result
     block_ref[...] = flat_ref[...].astype(BF16)
+
+
+def input_kernel(pieces, rows, where_ref, class_ref, x_ref, u_ref, label_ref, depth_grad_ref, one_ref, two_ref, kernel_ref, input_ref, x_buf, u_buf, halo_buf, flat_ref, class_buf, label_buf, kernel_buf, sems):
+    cols, sub, channels = halo_buf.shape
+    got_grad, got_kernel, got_x, got_u, got_label, got_class = fetches(
+        (depth_grad_ref, kernel_ref, x_ref.at[0], u_ref.at[0], label_ref, class_ref),
+        (halo_buf, kernel_buf, x_buf, u_buf, label_buf, class_buf),
+        sems,
+    )
+    even = where_ref[0] % 2 == 0
+    has_top = jnp.where(where_ref[0] > 0, 1.0, 0.0)
+    has_bottom = jnp.where(where_ref[0] < pieces - 1, 1.0, 0.0)
     one = one_ref[...].astype(F32)
     two = two_ref[...].astype(F32)
     top = jnp.where(even, two, one) * has_top
@@ -377,6 +382,7 @@
             pending = before + sums[1]
             before = sums[2]
         halo_buf[cols - 1, :, at] = pending
+    got_x.wait()
     got_u.wait()
     got_label.wait()
     got_class.wait()
@@ -384,8 +390,8 @@
     for col in range(cols):
         grads = column(u_buf, col, channels) * weight[:, col : col + 1]
         image = column(x_buf, col, channels)
-        flat2_ref[:, col * channels : (col + 1) * channels] = grads + jnp.where(image > 0, halo_buf[col, :rows, :], 0.0)
-    input_ref[...] = flat2_ref[...].astype(BF16)
+        flat_ref[:, col * channels : (col + 1) * channels] = grads + jnp.where(image > 0, halo_buf[col, :rows, :], 0.0)
+    input_ref[...] = flat_ref[...].astype(BF16)
 
 
 def call(body, ins, outs, scratch=(), megabytes=16):
@@ -397,7 +403,7 @@
     }
     return pl.pallas_call(
         body,
-        out_shape=[jax.ShapeDtypeStruct(shape, dtype) for _, shape, dtype in outs],
+        out_shape=[pltpu.HBM(shape, dtype) if s == "a" else jax.ShapeDtypeStruct(shape, dtype) for s, shape, dtype in outs],
         in_specs=[space[s] for s, _ in ins],
         out_specs=[space[s] for s, _, _ in outs],
         scratch_shapes=list(scratch),
@@ -506,10 +512,17 @@
             [("s", where), ("v", taps), ("v", lax.ppermute(taps, "slab", near)), ("v", norm)],
             fold_outs,
         )
+        leave, norm = lax.optimization_barrier((leave, norm))
         leave = lax.ppermute(leave, "slab", across)
     else:
         all_taps = lax.all_gather(taps, "slab", axis=0, tiled=True)
         stay, leave = call(functools.partial(fold_kernel, pieces), [("s", where), ("v", all_taps), ("v", norm)], fold_outs)
+    (block_out,) = call(
+        functools.partial(block_kernel, rows),
+        [("a", inputs), ("o", projected), ("v", norm), ("v", gain), ("v", shift)],
+        [("v", (rows, flat), BF16)],
+        [flat_buf, pltpu.VMEM((pixels, channels), F32), flat_f32, DMA((2,))],
+    )
     piece = -(-(share + 2 * lines) // copies)
     total = piece * copies
     (packed,) = call(
@@ -523,12 +536,11 @@
     gathered = lax.all_to_all(summed, "dp", 0, 0)
     halo_one = lax.ppermute(edge_one, "slab", near)
     halo_two = lax.ppermute(edge_two, "slab", far)
-    block_out, grad_input = call(
-        functools.partial(output_kernel, pieces, rows),
-        [("s", where), ("a", class_weights), ("a", inputs), ("a", upstream), ("a", label_lines), ("a", projected), ("v", norm), ("v", gain), ("v", shift), ("a", depth_grad), ("v", halo_one), ("v", halo_two), ("a", depth_kernel)],
-        [("v", (rows, flat), BF16), ("v", (rows, flat), BF16)],
-        [flat_buf, flat_buf, pltpu.VMEM((pixels, channels), F32), buf3, flat_f32, flat_f32, class_buf, label_buf, kernel_buf, DMA((7,))],
-        megabytes=16,
+    (grad_input,) = call(
+        functools.partial(input_kernel, pieces, rows),
+        [("s", where), ("a", class_weights), ("a", inputs), ("a", upstream), ("a", label_lines), ("a", depth_grad), ("v", halo_one), ("v", halo_two), ("a", depth_kernel)],
+        [("v", (rows, flat), BF16)],
+        [flat_buf, flat_buf, buf3, flat_f32, class_buf, label_buf, kernel_buf, DMA((6,))],
     )
     point_out, tap_out, gain_out, shift_out = call(
         functools.partial(unpack_kernel, pieces, batch),

time: 60.6 us -> 59.6 us (0.983)
  waiting for transfers between devices: 10.9 us -> 9.05 us
  local copies, waits for them, and re-layouts: 2.24 us -> 1.22 us
  Pallas kernels: 19 us -> 20 us
    ppermute x1, waiting for transfers between devices: 2.81 us -> 0.31 us  [local(): halo_two = lax.ppermute(edge_two, 'slab', far)]
    unnamed x10 -> x8, local copies, waits for them, and re-layouts: 1.03 us -> 0.02 us
    pallas_call x11 -> x12, Pallas kernels: 19 us -> 20 us  [call(): pl.pallas_call(body, out_shape=[pltpu.HBM(shape, dtype) if s == 'a' else...]
    all_to_all x1, waiting for transfers between devices: 0.01 us -> 0.81 us  [local(): gathered = lax.all_to_all(summed, 'dp', 0, 0)]
  transfers between devices with their start and end apart: 13 -> 13, of which waited for: 7 -> 7; matrix products, arithmetic and copies ran while one was open for 2% -> 2% of each run, Pallas kernels for 21% -> 24%
where the time goes in v1:
time: 59.6 us; the launch traced here: 59.1 us
  Pallas kernels  20 us (34%)
  blocking collectives  15.6 us (26%)
  starting transfers between devices  12.5 us (21%)
  waiting for transfers between devices  9.05 us (15%)
  local copies, waits for them, and re-layouts  1.22 us (2%)
  between operations  0.8 us (1%)
    pallas_call x12, Pallas kernels, call(): pl.pallas_call(body, out_shape=[pltpu.HBM(shape, dtype) if s == 'a' else...  20 us
    all_to_all x1, blocking collectives, local(): landed = lax.all_to_all(packed, 'dp', 0, 0)  15.6 us
    all_to_all x1, starting transfers between devices, local(): gathered = lax.all_to_all(summed, 'dp', 0, 0)  3.42 us
    ppermute x1, waiting for transfers between devices, local(): leave = lax.ppermute(leave, 'slab', across)  3.04 us
    ppermute x1, starting transfers between devices, local(): lax.ppermute(lax.dynamic_slice_in_dim(image, jnp.where(even, 0, rows - 1)...  2.69 us
    ppermute x3, waiting for transfers between devices, local(): lax.ppermute(stats, 'slab', pairs)  2.48 us
    ppermute x3, starting transfers between devices, local(): lax.ppermute(stats, 'slab', pairs)  2.12 us
    ppermute x1, starting transfers between devices, local(): came = lax.ppermute(leaving, 'slab', across)  1.43 us
  transfers between devices with their start and end apart: 13, of which 7 were waited for; matrix products, arithmetic and copies ran while one was open for 2% of the time, Pallas kernels for 24%

profile of v1, /device:TPU:0, one launch (start us, length us, event | category | flops | bytes accessed | tf_op | source)
XLA Modules:
  0.0 59.1 jit_solution(11390170266014999220)
XLA Ops:
  0.6 0.5 collective-permute-start
  1.1 1.2 %dynamic-slice_bitcast_fusion = bf16[1,34944]{1,0:T(2,128)(2,1)S(1)} fusion(bf16[1,6,34944]{2,1,0:T(8,128)(2,1)} %x_ref.5, s32[]{:T(128)S(6)} %select_n.13), kind=kLoop, calls=%fused_computation | loop fusion | bytes 139780 | tf_op jit(solution)/shard_map/dynamic_slice | solution.py:443
  2.4 2.7 %collective-permute-start.1 = (bf16[1,34944]{1,0:T(2,128)(2,1)S(1)}, bf16[1,34944]{1,0:T(2,128)(2,1)S(1)}, u32[]{:S(2)}, u32[]{:S(2)}) collective-permute-start(bf16[1,34944]{1,0:T(2,128)(2,1)S(1)} %dynamic-slice_bitcast_fusion), channel_id=1, source_target_pairs={{0,3},{1,2},{2,1},{3,0},{4,7},{5,6},{6,5},{7,4},{8,11},{9,10},{10,... | collective-permute-start | bytes 209672 | tf_op jit(solution)/shard_map/ppermute | solution.py:443
  5.0 4.6 %shard_map.127 = (f32[48,8,728]{2,1,0:T(8,128)S(1)}, f32[48,8,728]{2,1,0:T(8,128)S(1)}, f32[48,8,728]{2,1,0:T(8,128)S(1)}) custom-call(f32[3]{0:T(128)} %class_ref.3, bf16[1,6,34944]{2,1,0:T(8,128)(2,1)} %x_ref.5, bf16[1,6,34944]{2,1,0:T(8,128)(2,1)} %u_ref.3, s32[6,1,48]{2,1,0:T(1,128)} %bitcast.9, bf16[9,728]{1,0:T(8,128)(2,1)} %kernel_ref.5), custom_call_target="tpu_custom_call" | custom-call | tf_op jit(solution)/shard_map/pallas_call | solution.py:404
  9.6 2.8 %shard_map.128 = (bf16[384,768]{1,0:T(8,128)(2,1)S(1)}, f32[384,728]{1,0:T(8,128)S(1)}, f32[48,8,728]{2,1,0:T(8,128)}, f32[8,728]{1,0:T(8,128)S(1)}) custom-call(s32[1]{0:T(128)} %bitcast.where_ref, f32[48,8,728]{2,1,0:T(8,128)S(1)} %get-tuple-element.31.part_ref, f32[48,8,728]{2,1,0:T(8,128)S(1)} %get-tuple-element.32.own_ref, ...), custom_call_target="tpu_custom_call" | custom-call | tf_op jit(solution)/shard_map/pallas_call | solution.py:404
  12.4 0.1 collective-permute-start.2
  12.5 0.8 %collective-permute-start.5 = (f32[8,728]{1,0:T(8,128)S(1)}, f32[8,728]{1,0:T(8,128)S(1)}, u32[]{:S(2)}, u32[]{:S(2)}) collective-permute-start(f32[8,728]{1,0:T(8,128)S(1)} %get-tuple-element.36.refs_0_), channel_id=1, source_target_pairs={{0,3},{1,2},{2,1},{3,0},{4,7},{5,6},{6,5},{7,4},{8,11},{9,10},{10,... | collective-permute-start | bytes 69896 | tf_op jit(solution)/shard_map/ppermute | solution.py:461
  13.3 1.3 %collective-permute-start.4 = (f32[8,728]{1,0:T(8,128)S(1)}, f32[8,728]{1,0:T(8,128)S(1)}, u32[]{:S(2)}, u32[]{:S(2)}) collective-permute-start(f32[8,728]{1,0:T(8,128)S(1)} %get-tuple-element.36.refs_0_), channel_id=1, source_target_pairs={{0,2},{1,3},{2,0},{3,1},{4,6},{5,7},{6,4},{7,5},{8,10},{9,11},{10,... | collective-permute-start | bytes 69896 | tf_op jit(solution)/shard_map/ppermute | solution.py:461
  14.6 1.2 %collective-permute-done.5.refs_3_ = f32[8,728]{1,0:T(8,128)S(1)} collective-permute-done((f32[8,728]{1,0:T(8,128)S(1)}, f32[8,728]{1,0:T(8,128)S(1)}, u32[]{:S(2)}, u32[]{:S(2)}) %collective-permute-start.5) | collective-permute-done | bytes 23328 | tf_op jit(solution)/shard_map/ppermute | solution.py:461
  15.8 1.3 %collective-permute-done.4.refs_2_ = f32[8,728]{1,0:T(8,128)S(1)} collective-permute-done((f32[8,728]{1,0:T(8,128)S(1)}, f32[8,728]{1,0:T(8,128)S(1)}, u32[]{:S(2)}, u32[]{:S(2)}) %collective-permute-start.4) | collective-permute-done | bytes 23328 | tf_op jit(solution)/shard_map/ppermute | solution.py:461
  17.1 0.4 shard_map.129
  17.6 0.1 collective-permute-start.6
  17.6 0.8 %shard_map.130.own_ref = f32[728,728]{1,0:T(8,128)S(1)} custom-call(bf16[384,768]{1,0:T(8,128)(2,1)S(1)} %get-tuple-element.39.full_ref, bf16[384,768]{1,0:T(8,128)(2,1)S(1)} %get-tuple-element.35.depth_ref), custom_call_target="tpu_custom_call" | custom-call | tf_op jit(solution)/shard_map/pallas_call | solution.py:404
  18.5 1.2 %collective-permute-done.6.full_ref = bf16[384,768]{1,0:T(8,128)(2,1)S(1)} collective-permute-done((bf16[384,768]{1,0:T(8,128)(2,1)S(1)}, bf16[384,768]{1,0:T(8,128)(2,1)S(1)}, u32[]{:S(2)}, u32[]{:S(2)}) %collective-permute-start.6) | collective-permute-done | bytes 589856 | tf_op jit(solution)/shard_map/ppermute | solution.py:469
  19.6 1.0 %shard_map.131 = (f32[182,728]{1,0:T(8,128)S(1)}, bf16[182,728]{1,0:T(8,128)(2,1)S(1)}) custom-call(s32[1]{0:T(128)} %bitcast.where_ref, bf16[384,768]{1,0:T(8,128)(2,1)S(1)} %collective-permute-done.6.full_ref, bf16[384,768]{1,0:T(8,128)(2,1)S(1)} %collective-permute-done.2._.depth_ref, f32[728,728]{1,0:T(8,128)S(1)} %shard_map.130.own_ref), custom_call_target="tpu_custom_call" | custom-call | tf_op jit(solution)/shard_map/pallas_call | solution.py:404
  20.6 1.4 %collective-permute-start.10 = (bf16[182,728]{1,0:T(8,128)(2,1)S(1)}, bf16[182,728]{1,0:T(8,128)(2,1)S(1)}, u32[]{:S(2)}, u32[]{:S(2)}) collective-permute-start(bf16[182,728]{1,0:T(8,128)(2,1)S(1)} %get-tuple-element.49), channel_id=1, source_target_pairs={{0,2},{1,3},{2,0},{3,1},{4,6},{5,7},{6,4},{7,5},{8,10},{9,11},{10,... | collective-permute-start | bytes 794984 | tf_op jit(solution)/shard_map/ppermute | solution.py:499
  22.0 2.5 %shard_map.132 = (f32[48,8,728]{2,1,0:T(8,128)}, f32[16,728]{1,0:T(8,128)S(1)}, bf16[48,728]{1,0:T(8,128)(2,1)S(1)}, bf16[48,728]{1,0:T(8,128)(2,1)S(1)}) custom-call(s32[1]{0:T(128)} %bitcast.where_ref, bf16[384,768]{1,0:T(8,128)(2,1)S(1)} %get-tuple-element.39.full_ref, bf16[728,728]{1,0:T(8,128)(2,1)S(1)} %copy-done, f32[48,8,728]{2,1,0:T(8,128)S(1)} %copy-done.1), custom_call_target="tpu_custom_call" | custom-call | tf_op jit(solution)/shard_map/pallas_call | solution.py:404
  24.6 0.1 collective-permute-start.7
  24.6 1.2 %collective-permute-done.7.other_ref = f32[16,728]{1,0:T(8,128)S(1)} collective-permute-done((f32[16,728]{1,0:T(8,128)S(1)}, f32[16,728]{1,0:T(8,128)S(1)}, u32[]{:S(2)}, u32[]{:S(2)}) %collective-permute-start.7) | collective-permute-done | bytes 46624 | tf_op jit(solution)/shard_map/ppermute | solution.py:512
  25.9 0.1 shard_map.133
  26.0 0.7 %collective-permute-start.11 = (f32[3,728]{1,0:T(4,128)S(1)}, f32[3,728]{1,0:T(4,128)S(1)}, u32[]{:S(2)}, u32[]{:S(2)}) collective-permute-start(f32[3,728]{1,0:T(4,128)S(1)} %get-tuple-element.51), channel_id=1, source_target_pairs={{0,2},{1,3},{2,0},{3,1},{4,6},{5,7},{6,4},{7,5},{8,10},{9,11},{10,... | collective-permute-start | bytes 26216 | tf_op jit(solution)/shard_map/ppermute | solution.py:516
  26.7 3.0 %collective-permute-done.11.other_ref = f32[3,728]{1,0:T(4,128)S(1)} collective-permute-done((f32[3,728]{1,0:T(4,128)S(1)}, f32[3,728]{1,0:T(4,128)S(1)}, u32[]{:S(2)}, u32[]{:S(2)}) %collective-permute-start.11) | collective-permute-done | bytes 8768 | tf_op jit(solution)/shard_map/ppermute | solution.py:516
  29.7 0.1 shard_map.136
  29.9 15.6 %all_to_all.10.in_ref = bf16[8,24,728]{2,1,0:T(8,128)(2,1)S(1)} all-to-all(bf16[8,24,728]{2,1,0:T(8,128)(2,1)S(1)} %shard_map.136), channel_id=1, replica_groups=mesh['dp'=8,'slab'=4] {'dp'}, dimensions={0} | all-to-all | bytes 559104 | tf_op jit(solution)/shard_map/all_to_all | solution.py:534
  45.5 0.8 %shard_map.137 = bf16[8,24,728]{2,1,0:T(8,128)(2,1)} custom-call(bf16[8,24,728]{2,1,0:T(8,128)(2,1)S(1)} %all_to_all.10.in_ref), custom_call_target="tpu_custom_call" | custom-call | tf_op jit(solution)/shard_map/pallas_call | solution.py:404
  46.2 3.4 %all-to-all-start.1 = ((bf16[8,24,728]{2,1,0:T(8,128)(2,1)}), bf16[8,24,728]{2,1,0:T(8,128)(2,1)S(1)}, u32[]{:S(2)}, u32[]{:S(2)}) async-start(bf16[8,24,728]{2,1,0:T(8,128)(2,1)} %shard_map.137), calls=%async_computation.1 | async-start | bytes 589824 | tf_op jit(solution)/shard_map/all_to_all | solution.py:536
  49.8 1.3 %collective-permute-start.9 = (bf16[48,728]{1,0:T(8,128)(2,1)S(1)}, bf16[48,728]{1,0:T(8,128)(2,1)S(1)}, u32[]{:S(2)}, u32[]{:S(2)}) collective-permute-start(bf16[48,728]{1,0:T(8,128)(2,1)S(1)} %get-tuple-element.47), channel_id=1, source_target_pairs={{0,3},{1,2},{2,1},{3,0},{4,7},{5,6},{6,5},{7,4},{8,11},{9,10},{10,... | collective-permute-start | bytes 209672 | tf_op jit(solution)/shard_map/ppermute | solution.py:538
  51.0 2.5 %shard_map.134 = bf16[6,34944]{1,0:T(8,128)(2,1)} custom-call(bf16[1,6,34944]{2,1,0:T(8,128)(2,1)} %x_ref.5, f32[384,728]{1,0:T(8,128)S(1)} %get-tuple-element.34.proj_ref, f32[8,728]{1,0:T(8,128)S(1)} %get-tuple-element.44.norm_ref, f32[728]{0:T(1024)S(1)} %copy-done.2, f32[728]{0:T(1024)S(1)} %copy-done.3), custom_call_target="tpu_custom_call" | custom-call | tf_op jit(solution)/shard_map/pallas_call | solution.py:404
  53.5 0.3 collective-permute-done.9.two_ref
  53.8 3.6 %shard_map.135 = bf16[6,34944]{1,0:T(8,128)(2,1)} custom-call(s32[1]{0:T(128)} %bitcast.where_ref, f32[3]{0:T(128)} %class_ref.3, bf16[1,6,34944]{2,1,0:T(8,128)(2,1)} %x_ref.5, bf16[1,6,34944]{2,1,0:T(8,128)(2,1)} %u_ref.3, s32[6,1,48]{2,1,0:T(1,128)} %bitcast.10, f32[48,8,728]{2,1,0:T(8,128)} %get-tuple-element.45.depth_grad_ref, ...), custom_call_target="tpu_custom_call" | custom-call | tf_op jit(solution)/shard_map/pallas_call | solution.py:404
  57.5 0.8 %all-to-all-done.1.refs_0_ = bf16[8,24,728]{2,1,0:T(8,128)(2,1)S(1)} async-done(((bf16[8,24,728]{2,1,0:T(8,128)(2,1)}), bf16[8,24,728]{2,1,0:T(8,128)(2,1)S(1)}, u32[]{:S(2)}, u32[]{:S(2)}) %all-to-all-start.1) | async-done | bytes 279584 | tf_op jit(solution)/shard_map/all_to_all | solution.py:536
  58.3 0.9 %shard_map.138 = (f32[182,728]{1,0:T(8,128)}, f32[9,182]{1,0:T(8,128)}, f32[182]{0:T(256)}, f32[182]{0:T(256)}) custom-call(bf16[8,24,728]{2,1,0:T(8,128)(2,1)S(1)} %all-to-all-done.1.refs_0_), custom_call_target="tpu_custom_call" | custom-call | tf_op jit(solution)/shard_map/pallas_call | solution.py:404
  (16 shorter events, 0.1 us)
Async XLA Ops:
  0.6 9.0 %collective-permute-start = (bf16[1,6,34944]{2,1,0:T(8,128)(2,1)}, bf16[1,6,34944]{2,1,0:T(8,128)(2,1)S(1)}, u32[]{:S(2)}, u32[]{:S(2)}) collective-permute-start(bf16[1,6,34944]{2,1,0:T(8,128)(2,1)} %x_ref.5), channel_id=1, source_target_pairs={{0,1},{1,0},{2,3},{3,2},{4,5},{5,4},{6,7},{7,6},{8,9},{9,8},{10,11... | collective-permute-start | bytes 1257992 | tf_op jit(solution)/shard_map/ppermute | solution.py:442
  2.4 7.3 %collective-permute-start.1 = (bf16[1,34944]{1,0:T(2,128)(2,1)S(1)}, bf16[1,34944]{1,0:T(2,128)(2,1)S(1)}, u32[]{:S(2)}, u32[]{:S(2)}) collective-permute-start(bf16[1,34944]{1,0:T(2,128)(2,1)S(1)} %dynamic-slice_bitcast_fusion), channel_id=1, source_target_pairs={{0,3},{1,2},{2,1},{3,0},{4,7},{5,6},{6,5},{7,4},{8,11},{9,10},{10,... | collective-permute-start | bytes 209672 | tf_op jit(solution)/shard_map/ppermute | solution.py:443
  9.6 7.5 %copy-start.2 = (f32[728]{0:T(1024)S(1)}, f32[728]{0:T(1024)}, u32[]{:S(2)}) copy-start(f32[728]{0:T(1024)} %gain_ref.3) | copy-start | bytes 8740
  12.4 4.7 %collective-permute-start.2 = (bf16[384,768]{1,0:T(8,128)(2,1)S(1)}, bf16[384,768]{1,0:T(8,128)(2,1)S(1)}, u32[]{:S(2)}, u32[]{:S(2)}) collective-permute-start(bf16[384,768]{1,0:T(8,128)(2,1)S(1)} %get-tuple-element.35.depth_ref), channel_id=1, source_target_pairs={{0,1},{1,0},{2,3},{3,2},{4,5},{5,4},{6,7},{7,6},{8,9},{9,8},{10,11... | collective-permute-start | bytes 1769480 | tf_op jit(solution)/shard_map/ppermute | solution.py:457
  12.5 3.3 %collective-permute-start.5 = (f32[8,728]{1,0:T(8,128)S(1)}, f32[8,728]{1,0:T(8,128)S(1)}, u32[]{:S(2)}, u32[]{:S(2)}) collective-permute-start(f32[8,728]{1,0:T(8,128)S(1)} %get-tuple-element.36.refs_0_), channel_id=1, source_target_pairs={{0,3},{1,2},{2,1},{3,0},{4,7},{5,6},{6,5},{7,4},{8,11},{9,10},{10,... | collective-permute-start | bytes 69896 | tf_op jit(solution)/shard_map/ppermute | solution.py:461
  13.3 3.8 %collective-permute-start.4 = (f32[8,728]{1,0:T(8,128)S(1)}, f32[8,728]{1,0:T(8,128)S(1)}, u32[]{:S(2)}, u32[]{:S(2)}) collective-permute-start(f32[8,728]{1,0:T(8,128)S(1)} %get-tuple-element.36.refs_0_), channel_id=1, source_target_pairs={{0,2},{1,3},{2,0},{3,1},{4,6},{5,7},{6,4},{7,5},{8,10},{9,11},{10,... | collective-permute-start | bytes 69896 | tf_op jit(solution)/shard_map/ppermute | solution.py:461
  14.6 2.5 %collective-permute-start.3 = (f32[8,728]{1,0:T(8,128)S(1)}, f32[8,728]{1,0:T(8,128)S(1)}, u32[]{:S(2)}, u32[]{:S(2)}) collective-permute-start(f32[8,728]{1,0:T(8,128)S(1)} %get-tuple-element.36.refs_0_), channel_id=1, source_target_pairs={{0,1},{1,0},{2,3},{3,2},{4,5},{5,4},{6,7},{7,6},{8,9},{9,8},{10,11... | collective-permute-start | bytes 69896 | tf_op jit(solution)/shard_map/ppermute | solution.py:461
  17.6 2.1 %collective-permute-start.6 = (bf16[384,768]{1,0:T(8,128)(2,1)S(1)}, bf16[384,768]{1,0:T(8,128)(2,1)S(1)}, u32[]{:S(2)}, u32[]{:S(2)}) collective-permute-start(bf16[384,768]{1,0:T(8,128)(2,1)S(1)} %get-tuple-element.39.full_ref), channel_id=1, source_target_pairs={{0,1},{1,0},{2,3},{3,2},{4,5},{5,4},{6,7},{7,6},{8,9},{9,8},{10,11... | collective-permute-start | bytes 1769480 | tf_op jit(solution)/shard_map/ppermute | solution.py:469
  18.4 3.6 %copy-start = (bf16[728,728]{1,0:T(8,128)(2,1)S(1)}, bf16[728,728]{1,0:T(8,128)(2,1)}, u32[]{:S(2)}) copy-start(bf16[728,728]{1,0:T(8,128)(2,1)} %point_ref.3) | copy-start | bytes 3179908
  18.4 3.6 %copy-start.1 = (f32[48,8,728]{2,1,0:T(8,128)S(1)}, f32[48,8,728]{2,1,0:T(8,128)}, u32[]{:S(2)}) copy-start(f32[48,8,728]{2,1,0:T(8,128)} %get-tuple-element.40.active_ref) | copy-start | bytes 3354628
  20.6 9.1 %collective-permute-start.10 = (bf16[182,728]{1,0:T(8,128)(2,1)S(1)}, bf16[182,728]{1,0:T(8,128)(2,1)S(1)}, u32[]{:S(2)}, u32[]{:S(2)}) collective-permute-start(bf16[182,728]{1,0:T(8,128)(2,1)S(1)} %get-tuple-element.49), channel_id=1, source_target_pairs={{0,2},{1,3},{2,0},{3,1},{4,6},{5,7},{6,4},{7,5},{8,10},{9,11},{10,... | collective-permute-start | bytes 794984 | tf_op jit(solution)/shard_map/ppermute | solution.py:499
  24.6 1.3 %collective-permute-start.7 = (f32[16,728]{1,0:T(8,128)S(1)}, f32[16,728]{1,0:T(8,128)S(1)}, u32[]{:S(2)}, u32[]{:S(2)}) collective-permute-start(f32[16,728]{1,0:T(8,128)S(1)} %get-tuple-element.41.taps_ref), channel_id=1, source_target_pairs={{0,1},{1,0},{2,3},{3,2},{4,5},{5,4},{6,7},{7,6},{8,9},{9,8},{10,11... | collective-permute-start | bytes 139784 | tf_op jit(solution)/shard_map/ppermute | solution.py:512
  26.0 3.8 %collective-permute-start.11 = (f32[3,728]{1,0:T(4,128)S(1)}, f32[3,728]{1,0:T(4,128)S(1)}, u32[]{:S(2)}, u32[]{:S(2)}) collective-permute-start(f32[3,728]{1,0:T(4,128)S(1)} %get-tuple-element.51), channel_id=1, source_target_pairs={{0,2},{1,3},{2,0},{3,1},{4,6},{5,7},{6,4},{7,5},{8,10},{9,11},{10,... | collective-permute-start | bytes 26216 | tf_op jit(solution)/shard_map/ppermute | solution.py:516
  29.7 21.3 %copy-start.3 = (f32[728]{0:T(1024)S(1)}, f32[728]{0:T(1024)}, u32[]{:S(2)}) copy-start(f32[728]{0:T(1024)} %shift_ref.1) | copy-start | bytes 8740
  46.2 12.0 %all-to-all-start.1 = ((bf16[8,24,728]{2,1,0:T(8,128)(2,1)}), bf16[8,24,728]{2,1,0:T(8,128)(2,1)S(1)}, u32[]{:S(2)}, u32[]{:S(2)}) async-start(bf16[8,24,728]{2,1,0:T(8,128)(2,1)} %shard_map.137), calls=%async_computation.1 | async-start | bytes 589824 | tf_op jit(solution)/shard_map/all_to_all | solution.py:536
  49.7 3.8 %collective-permute-start.8 = (bf16[48,728]{1,0:T(8,128)(2,1)S(1)}, bf16[48,728]{1,0:T(8,128)(2,1)S(1)}, u32[]{:S(2)}, u32[]{:S(2)}) collective-permute-start(bf16[48,728]{1,0:T(8,128)(2,1)S(1)} %get-tuple-element.46), channel_id=1, source_target_pairs={{0,1},{1,0},{2,3},{3,2},{4,5},{5,4},{6,7},{7,6},{8,9},{9,8},{10,11... | collective-permute-start | bytes 209672 | tf_op jit(solution)/shard_map/ppermute | solution.py:537
  49.8 4.1 %collective-permute-start.9 = (bf16[48,728]{1,0:T(8,128)(2,1)S(1)}, bf16[48,728]{1,0:T(8,128)(2,1)S(1)}, u32[]{:S(2)}, u32[]{:S(2)}) collective-permute-start(bf16[48,728]{1,0:T(8,128)(2,1)S(1)} %get-tuple-element.47), channel_id=1, source_target_pairs={{0,3},{1,2},{2,1},{3,0},{4,7},{5,6},{6,5},{7,4},{8,11},{9,10},{10,... | collective-permute-start | bytes 209672 | tf_op jit(solution)/shard_map/ppermute | solution.py:538

commit v2 on v1

--- a/solution.py
+++ b/solution.py
@@ -23,12 +23,15 @@
     return [(start, min(LANES, width - start)) for start in range(0, width, LANES)]
 
 
-def column(ref, col, channels):
+def column(ref, col, channels, scale=None):
     start = col * channels
     base = start // LANES * LANES
     off = start - base
     end = min(ref.shape[1], base + round_up(off + channels, LANES))
-    return ref[:, base:end].astype(F32)[:, off : off + channels]
+    values = ref[:, base:end].astype(F32)
+    if scale is not None:
+        values = values * jnp.concatenate([scale] * ((end - base) // LANES), axis=1)
+    return values[:, off : off + channels]
 
 
 def pixel_weights(class_ref, label_ref):
@@ -39,6 +42,11 @@
     return weight
 
 
+def spread_weights(ref, weight):
+    for col in range(ref.shape[0]):
+        ref[col] = jnp.broadcast_to(weight[:, col : col + 1], ref.shape[1:])
+
+
 def fetches(sources, buffers, sems):
     copies = [pltpu.make_async_copy(s, b, sems.at[i]) for i, (s, b) in enumerate(zip(sources, buffers))]
     for copy in copies:
@@ -46,7 +54,7 @@
     return copies
 
 
-def prepare_kernel(class_ref, x_ref, u_ref, label_ref, kernel_ref, active_ref, part_ref, grad_ref, class_buf, x_buf, u_buf, label_buf, kernel_buf, sems):
+def prepare_kernel(class_ref, x_ref, u_ref, label_ref, kernel_ref, active_ref, part_ref, grad_ref, class_buf, x_buf, u_buf, label_buf, kernel_buf, weight_buf, sems):
     rows, _, cols = label_buf.shape
     sub, channels = grad_ref.shape[1:]
     got_x, got_kernel, got_u, got_label, got_class = fetches(
@@ -75,34 +83,33 @@
     got_u.wait()
     got_label.wait()
     got_class.wait()
-    weight = pixel_weights(class_buf, label_buf)
+    spread_weights(weight_buf, pixel_weights(class_buf, label_buf))
     for col in range(cols):
-        grad_ref[col] = jnp.concatenate([column(u_buf, col, channels) * weight[:, col : col + 1], below], axis=0)
-
-
-def forward_kernel(pieces, rows, where_ref, part_ref, own_ref, one_ref, two_ref, kernel_ref, point_ref, grad_ref, depth_ref, proj_ref, active_ref, stats_ref, part_buf, active_buf, halo_buf, point_buf, kernel_buf, sems):
+        grad_ref[col] = jnp.concatenate([column(u_buf, col, channels, weight_buf[col]), below], axis=0)
+
+
+def forward_kernel(pieces, rows, where_ref, part_ref, own_ref, one_ref, two_ref, kernel_ref, point_ref, grad_ref, depth_ref, proj_ref, active_ref, stats_ref, part_buf, halo_buf, line_buf):
     cols, sub, channels = part_buf.shape
-    got_kernel, got_point = fetches((kernel_ref, point_ref), (kernel_buf, point_buf), sems)
-    put_active = pltpu.make_async_copy(active_buf, active_ref, sems.at[2])
     even = where_ref[0] % 2 == 0
     near_line = jnp.where(even, rows, sub - 1)
     far_line = jnp.where(even, sub - 1, rows)
     far_line = jnp.where((where_ref[0] == 0) | (where_ref[0] == pieces - 1), sub, far_line)
+    line_buf[...] = two_ref[...].astype(F32)
     for col in range(cols):
         start = col * channels
         base = start // LANES * LANES
         off = start - base
-        end = min(two_ref.shape[1], base + round_up(off + channels, LANES))
+        end = min(one_ref.shape[2], base + round_up(off + channels, LANES))
         near = one_ref[0, :, base:end].astype(F32)
         one = jnp.where(even, near[:1], near[rows - 1 :])
-        two = two_ref[:, base:end].astype(F32)
+        parts = [line_buf[t : t + 1, :] for t in range(base // LANES, -(-end // LANES))]
+        two = jnp.concatenate(parts, axis=1)[:, : end - base]
         line = lax.broadcasted_iota(jnp.int32, (sub, end - base), 0)
         lines = jnp.maximum(jnp.where(line == near_line, one, jnp.where(line == far_line, two, 0.0)), 0.0)
         halo_buf[col] = lines[:, off : off + channels]
-    got_kernel.wait()
     line = lax.broadcasted_iota(jnp.int32, (sub, channels), 0)
     wide = [
-        jnp.where(line == sub - 1, kernel_buf[j : j + 1, :].astype(F32), kernel_buf[6 + j : 7 + j, :].astype(F32))
+        jnp.where(line == sub - 1, kernel_ref[j : j + 1, :].astype(F32), kernel_ref[6 + j : 7 + j, :].astype(F32))
         for j in range(3)
     ]
     for start, width in tiles(channels):
@@ -119,18 +126,16 @@
         pending = before
         for col in range(cols):
             halo = halo_buf[col, :, at]
-            active_buf[col, :, at] = own_ref[col, :, at] + halo
+            active_ref[col, :, at] = own_ref[col, :, at] + halo
             if col:
                 finish(col - 1, pending + taps[2] * halo)
             pending = before + taps[1] * halo
             before = taps[0] * halo
         finish(cols - 1, pending)
-    put_active.start()
     depth = part_buf[...].reshape(cols * sub, channels).astype(BF16)
     depth_ref[:, :channels] = depth
     depth_ref[:, channels:] = jnp.zeros((cols * sub, depth_ref.shape[1] - channels), BF16)
-    got_point.wait()
-    proj_ref[...] = jnp.dot(depth, point_buf[...], preferred_element_type=F32)
+    proj_ref[...] = jnp.dot(depth, point_ref[...], preferred_element_type=F32)
     count = rows * cols
     for start, width in tiles(channels):
         at = pl.ds(start, width)
@@ -144,7 +149,6 @@
         stats_ref[2:3, at] = jnp.sum(grads, axis=0, keepdims=True)
         stats_ref[3:4, at] = jnp.sum(grads * deviation, axis=0, keepdims=True)
         stats_ref[4:SUB, at] = jnp.zeros((SUB - 4, width), F32)
-    put_active.wait()
 
 
 def paired_sum(values):
@@ -346,7 +350,7 @@
     block_ref[...] = flat_ref[...].astype(BF16)
 
 
-def input_kernel(pieces, rows, where_ref, class_ref, x_ref, u_ref, label_ref, depth_grad_ref, one_ref, two_ref, kernel_ref, input_ref, x_buf, u_buf, halo_buf, flat_ref, class_buf, label_buf, kernel_buf, sems):
+def input_kernel(pieces, rows, where_ref, class_ref, x_ref, u_ref, label_ref, depth_grad_ref, one_ref, two_ref, kernel_ref, input_ref, x_buf, u_buf, halo_buf, flat_ref, class_buf, label_buf, kernel_buf, weight_buf, sems):
     cols, sub, channels = halo_buf.shape
     got_grad, got_kernel, got_x, got_u, got_label, got_class = fetches(
         (depth_grad_ref, kernel_ref, x_ref.at[0], u_ref.at[0], label_ref, class_ref),
@@ -386,9 +390,9 @@
     got_u.wait()
     got_label.wait()
     got_class.wait()
-    weight = pixel_weights(class_buf, label_buf)
+    spread_weights(weight_buf, pixel_weights(class_buf, label_buf))
     for col in range(cols):
-        grads = column(u_buf, col, channels) * weight[:, col : col + 1]
+        grads = column(u_buf, col, channels, weight_buf[col])
         image = column(x_buf, col, channels)
         flat_ref[:, col * channels : (col + 1) * channels] = grads + jnp.where(image > 0, halo_buf[col, :rows, :], 0.0)
     input_ref[...] = flat_ref[...].astype(BF16)
@@ -437,22 +441,24 @@
     kernel_buf = pltpu.VMEM(depth_kernel.shape, BF16)
     label_buf = pltpu.VMEM((rows, 1, cols), labels.dtype)
     label_lines = jnp.transpose(labels, (1, 0, 2))
+    weight_buf = pltpu.VMEM((cols, rows, LANES), F32)
     class_buf = pltpu.SMEM(class_weights.shape, F32)
 
     one = lax.ppermute(inputs, "slab", near)
-    two = lax.ppermute(lax.dynamic_slice_in_dim(image, jnp.where(even, 0, rows - 1), 1, 0), "slab", far)
+    edge = jnp.where(even, image[0], image[rows - 1])
+    two = lax.ppermute(jnp.pad(edge, (0, -flat % LANES)).reshape(-1, LANES), "slab", far)
     own, part, grad_out = call(
         prepare_kernel,
         [("a", class_weights), ("a", inputs), ("a", upstream), ("a", label_lines), ("a", depth_kernel)],
         [("v", lane3, F32), ("v", lane3, F32), ("v", lane3, F32)],
-        [class_buf, flat_buf, flat_buf, label_buf, kernel_buf, DMA((5,))],
+        [class_buf, flat_buf, flat_buf, label_buf, kernel_buf, weight_buf, DMA((5,))],
         megabytes=16,
     )
     depth, projected, active, stats = call(
         functools.partial(forward_kernel, pieces, rows),
-        [("s", where), ("v", part), ("v", own), ("v", one), ("v", two), ("a", depth_kernel), ("a", point_weight), ("v", grad_out)],
-        [("v", (pixels, padded), BF16), ("v", (pixels, channels), F32), ("a", lane3, F32), ("v", (SUB, channels), F32)],
-        [buf3, buf3, buf3, point_buf, kernel_buf, DMA((3,))],
+        [("s", where), ("v", part), ("v", own), ("v", one), ("v", two), ("v", depth_kernel), ("v", point_weight), ("v", grad_out)],
+        [("v", (pixels, padded), BF16), ("v", (pixels, channels), F32), ("v", lane3, F32), ("v", (SUB, channels), F32)],
+        [buf3, buf3, pltpu.VMEM(two.shape, F32)],
     )
     other_depth = lax.ppermute(depth, "slab", near)
     across = [(i, i ^ 2) for i in range(pieces)]
@@ -540,7 +546,7 @@
         functools.partial(input_kernel, pieces, rows),
         [("s", where), ("a", class_weights), ("a", inputs), ("a", upstream), ("a", label_lines), ("a", depth_grad), ("v", halo_one), ("v", halo_two), ("a", depth_kernel)],
         [("v", (rows, flat), BF16)],
-        [flat_buf, flat_buf, buf3, flat_f32, class_buf, label_buf, kernel_buf, DMA((6,))],
+        [flat_buf, flat_buf, buf3, flat_f32, class_buf, label_buf, kernel_buf, weight_buf, DMA((6,))],
     )
     point_out, tap_out, gain_out, shift_out = call(
         functools.partial(unpack_kernel, pieces, batch),

time: 59.6 us -> 57.7 us (0.968)
  Pallas kernels: 20 us -> 17 us
  other arithmetic: 0 us -> 1.71 us
  local copies, waits for them, and re-layouts: 1.22 us -> 0.02 us
  waiting for transfers between devices: 9.05 us -> 10.1 us
    pallas_call x12, Pallas kernels: 20 us -> 17 us  [call(): pl.pallas_call(body, out_shape=[pltpu.HBM(shape, dtype) if s == 'a' else...]
    select_n x0 -> x1, other arithmetic: none -> 1.71 us  [local(): edge = jnp.where(even, image[0], image[rows - 1])]
    dynamic_slice x1 -> x0, local copies, waits for them, and re-layouts: 1.2 us -> none  [local(): lax.dynamic_slice_in_dim(image, jnp.where(even, 0, rows - 1), 1, 0)]
    ppermute x3, waiting for transfers between devices: 2.48 us -> 3.12 us  [local(): lax.ppermute(stats, 'slab', pairs)]
    ppermute x1, starting transfers between devices: 0.72 us -> 1.36 us  [local(): leave = lax.ppermute(leave, 'slab', across)]
    ppermute x1, starting transfers between devices: 1.43 us -> 0.79 us  [local(): came = lax.ppermute(leaving, 'slab', across)]
  transfers between devices with their start and end apart: 13 -> 13, of which waited for: 7 -> 7; matrix products, arithmetic and copies ran while one was open for 2% -> 3% of each run, Pallas kernels for 24% -> 21%
where the time goes in v2:
time: 57.7 us; the launch traced here: 57.3 us
  Pallas kernels  17 us (29%)
  blocking collectives  15.5 us (27%)
  starting transfers between devices  12.2 us (21%)
  waiting for transfers between devices  10.1 us (18%)
  other arithmetic  1.71 us (3%)
  between operations  0.81 us (1%)
    pallas_call x12, Pallas kernels, call(): pl.pallas_call(body, out_shape=[pltpu.HBM(shape, dtype) if s == 'a' else...  17 us
    all_to_all x1, blocking collectives, local(): landed = lax.all_to_all(packed, 'dp', 0, 0)  15.5 us
    all_to_all x1, starting transfers between devices, local(): gathered = lax.all_to_all(summed, 'dp', 0, 0)  3.42 us
    ppermute x3, waiting for transfers between devices, local(): lax.ppermute(stats, 'slab', pairs)  3.12 us
    ppermute x1, waiting for transfers between devices, local(): leave = lax.ppermute(leave, 'slab', across)  3.04 us
    ppermute x1, starting transfers between devices, local(): lax.ppermute(jnp.pad(edge, (0, -flat % LANES)).reshape(-1, LANES), 'slab'...  2.71 us
    ppermute x3, starting transfers between devices, local(): lax.ppermute(stats, 'slab', pairs)  2.08 us
    select_n x1, other arithmetic, local(): edge = jnp.where(even, image[0], image[rows - 1])  1.71 us
  transfers between devices with their start and end apart: 13, of which 7 were waited for; matrix products, arithmetic and copies ran while one was open for 3% of the time, Pallas kernels for 21%

profile of v2, /device:TPU:0, one launch (start us, length us, event | category | flops | bytes accessed | tf_op | source)
XLA Modules:
  0.0 57.3 jit_solution(16368495906460046332)
XLA Ops:
  0.7 0.5 collective-permute-start
  1.2 1.7 %fusion = bf16[34944]{0:T(1024)(128)(2,1)S(1)} fusion(pred[]{:T(512)S(6)} %eq.5, bf16[1,6,34944]{2,1,0:T(8,128)(2,1)} %x_ref.5), kind=kLoop, calls=%fused_computation.1 | loop fusion | flops 34944 | bytes 209665 | tf_op jit(solution)/shard_map/jit(_where)/select_n | solution.py:448
  2.9 2.7 %collective-permute-start.1 = (bf16[273,128]{1,0:T(8,128)(2,1)S(1)}, bf16[273,128]{1,0:T(8,128)(2,1)S(1)}, u32[]{:S(2)}, u32[]{:S(2)}) collective-permute-start(bf16[273,128]{1,0:T(8,128)(2,1)S(1)} %bitcast.8), channel_id=1, source_target_pairs={{0,3},{1,2},{2,1},{3,0},{4,7},{5,6},{6,5},{7,4},{8,11},{9,10},{10,... | collective-permute-start | bytes 209672 | tf_op jit(solution)/shard_map/ppermute | solution.py:449
  5.6 2.6 %shard_map.127 = (f32[48,8,728]{2,1,0:T(8,128)S(1)}, f32[48,8,728]{2,1,0:T(8,128)S(1)}, f32[48,8,728]{2,1,0:T(8,128)S(1)}) custom-call(f32[3]{0:T(128)} %class_ref.3, bf16[1,6,34944]{2,1,0:T(8,128)(2,1)} %x_ref.5, bf16[1,6,34944]{2,1,0:T(8,128)(2,1)} %u_ref.3, s32[6,1,48]{2,1,0:T(1,128)} %bitcast.9, bf16[9,728]{1,0:T(8,128)(2,1)} %kernel_ref.5), custom_call_target="tpu_custom_call" | custom-call | tf_op jit(solution)/shard_map/pallas_call | solution.py:408
  8.2 1.8 %shard_map.128 = (bf16[384,768]{1,0:T(8,128)(2,1)S(1)}, f32[384,728]{1,0:T(8,128)S(1)}, f32[48,8,728]{2,1,0:T(8,128)S(1)}, f32[8,728]{1,0:T(8,128)S(1)}) custom-call(s32[1]{0:T(128)} %bitcast.where_ref, f32[48,8,728]{2,1,0:T(8,128)S(1)} %get-tuple-element.31.part_ref, f32[48,8,728]{2,1,0:T(8,128)S(1)} %get-tuple-element.32.own_ref, ...), custom_call_target="tpu_custom_call" | custom-call | tf_op jit(solution)/shard_map/pallas_call | solution.py:408
  10.1 0.1 collective-permute-start.2
  10.2 1.4 %collective-permute-start.5 = (f32[8,728]{1,0:T(8,128)S(1)}, f32[8,728]{1,0:T(8,128)S(1)}, u32[]{:S(2)}, u32[]{:S(2)}) collective-permute-start(f32[8,728]{1,0:T(8,128)S(1)} %get-tuple-element.36.refs_0_), channel_id=1, source_target_pairs={{0,3},{1,2},{2,1},{3,0},{4,7},{5,6},{6,5},{7,4},{8,11},{9,10},{10,... | collective-permute-start | bytes 69896 | tf_op jit(solution)/shard_map/ppermute | solution.py:467
  11.6 0.7 %collective-permute-start.4 = (f32[8,728]{1,0:T(8,128)S(1)}, f32[8,728]{1,0:T(8,128)S(1)}, u32[]{:S(2)}, u32[]{:S(2)}) collective-permute-start(f32[8,728]{1,0:T(8,128)S(1)} %get-tuple-element.36.refs_0_), channel_id=1, source_target_pairs={{0,2},{1,3},{2,0},{3,1},{4,6},{5,7},{6,4},{7,5},{8,10},{9,11},{10,... | collective-permute-start | bytes 69896 | tf_op jit(solution)/shard_map/ppermute | solution.py:467
  12.3 1.2 %collective-permute-done.5.refs_3_ = f32[8,728]{1,0:T(8,128)S(1)} collective-permute-done((f32[8,728]{1,0:T(8,128)S(1)}, f32[8,728]{1,0:T(8,128)S(1)}, u32[]{:S(2)}, u32[]{:S(2)}) %collective-permute-start.5) | collective-permute-done | bytes 23328 | tf_op jit(solution)/shard_map/ppermute | solution.py:467
  13.5 1.9 %collective-permute-done.4.refs_2_ = f32[8,728]{1,0:T(8,128)S(1)} collective-permute-done((f32[8,728]{1,0:T(8,128)S(1)}, f32[8,728]{1,0:T(8,128)S(1)}, u32[]{:S(2)}, u32[]{:S(2)}) %collective-permute-start.4) | collective-permute-done | bytes 23328 | tf_op jit(solution)/shard_map/ppermute | solution.py:467
  15.4 0.4 shard_map.129
  16.0 0.8 %shard_map.130.own_ref = f32[728,728]{1,0:T(8,128)S(1)} custom-call(bf16[384,768]{1,0:T(8,128)(2,1)S(1)} %get-tuple-element.39.full_ref, bf16[384,768]{1,0:T(8,128)(2,1)S(1)} %get-tuple-element.35.depth_ref), custom_call_target="tpu_custom_call" | custom-call | tf_op jit(solution)/shard_map/pallas_call | solution.py:408
  16.7 1.2 %collective-permute-done.6.full_ref = bf16[384,768]{1,0:T(8,128)(2,1)S(1)} collective-permute-done((bf16[384,768]{1,0:T(8,128)(2,1)S(1)}, bf16[384,768]{1,0:T(8,128)(2,1)S(1)}, u32[]{:S(2)}, u32[]{:S(2)}) %collective-permute-start.6) | collective-permute-done | bytes 589856 | tf_op jit(solution)/shard_map/ppermute | solution.py:475
  17.9 1.0 %shard_map.131 = (f32[182,728]{1,0:T(8,128)S(1)}, bf16[182,728]{1,0:T(8,128)(2,1)S(1)}) custom-call(s32[1]{0:T(128)} %bitcast.where_ref, bf16[384,768]{1,0:T(8,128)(2,1)S(1)} %collective-permute-done.6.full_ref, bf16[384,768]{1,0:T(8,128)(2,1)S(1)} %collective-permute-done.2._.depth_ref, f32[728,728]{1,0:T(8,128)S(1)} %shard_map.130.own_ref), custom_call_target="tpu_custom_call" | custom-call | tf_op jit(solution)/shard_map/pallas_call | solution.py:408
  18.9 0.8 %collective-permute-start.10 = (bf16[182,728]{1,0:T(8,128)(2,1)S(1)}, bf16[182,728]{1,0:T(8,128)(2,1)S(1)}, u32[]{:S(2)}, u32[]{:S(2)}) collective-permute-start(bf16[182,728]{1,0:T(8,128)(2,1)S(1)} %get-tuple-element.49), channel_id=1, source_target_pairs={{0,2},{1,3},{2,0},{3,1},{4,6},{5,7},{6,4},{7,5},{8,10},{9,11},{10,... | collective-permute-start | bytes 794984 | tf_op jit(solution)/shard_map/ppermute | solution.py:505
  19.7 2.5 %shard_map.132 = (f32[48,8,728]{2,1,0:T(8,128)}, f32[16,728]{1,0:T(8,128)S(1)}, bf16[48,728]{1,0:T(8,128)(2,1)S(1)}, bf16[48,728]{1,0:T(8,128)(2,1)S(1)}) custom-call(s32[1]{0:T(128)} %bitcast.where_ref, bf16[384,768]{1,0:T(8,128)(2,1)S(1)} %get-tuple-element.39.full_ref, bf16[728,728]{1,0:T(8,128)(2,1)S(1)} %copy-done, ...), custom_call_target="tpu_custom_call" | custom-call | tf_op jit(solution)/shard_map/pallas_call | solution.py:408
  22.2 0.1 collective-permute-start.7
  22.3 1.2 %collective-permute-done.7.other_ref = f32[16,728]{1,0:T(8,128)S(1)} collective-permute-done((f32[16,728]{1,0:T(8,128)S(1)}, f32[16,728]{1,0:T(8,128)S(1)}, u32[]{:S(2)}, u32[]{:S(2)}) %collective-permute-start.7) | collective-permute-done | bytes 46624 | tf_op jit(solution)/shard_map/ppermute | solution.py:518
  23.5 0.1 shard_map.133
  23.7 1.4 %collective-permute-start.11 = (f32[3,728]{1,0:T(4,128)S(1)}, f32[3,728]{1,0:T(4,128)S(1)}, u32[]{:S(2)}, u32[]{:S(2)}) collective-permute-start(f32[3,728]{1,0:T(4,128)S(1)} %get-tuple-element.51), channel_id=1, source_target_pairs={{0,2},{1,3},{2,0},{3,1},{4,6},{5,7},{6,4},{7,5},{8,10},{9,11},{10,... | collective-permute-start | bytes 26216 | tf_op jit(solution)/shard_map/ppermute | solution.py:522
  25.0 3.0 %collective-permute-done.11.other_ref = f32[3,728]{1,0:T(4,128)S(1)} collective-permute-done((f32[3,728]{1,0:T(4,128)S(1)}, f32[3,728]{1,0:T(4,128)S(1)}, u32[]{:S(2)}, u32[]{:S(2)}) %collective-permute-start.11) | collective-permute-done | bytes 8768 | tf_op jit(solution)/shard_map/ppermute | solution.py:522
  28.1 0.1 shard_map.136
  28.2 15.5 %all_to_all.10.in_ref = bf16[8,24,728]{2,1,0:T(8,128)(2,1)S(1)} all-to-all(bf16[8,24,728]{2,1,0:T(8,128)(2,1)S(1)} %shard_map.136), channel_id=1, replica_groups=mesh['dp'=8,'slab'=4] {'dp'}, dimensions={0} | all-to-all | bytes 559104 | tf_op jit(solution)/shard_map/all_to_all | solution.py:540
  43.6 0.8 %shard_map.137 = bf16[8,24,728]{2,1,0:T(8,128)(2,1)} custom-call(bf16[8,24,728]{2,1,0:T(8,128)(2,1)S(1)} %all_to_all.10.in_ref), custom_call_target="tpu_custom_call" | custom-call | tf_op jit(solution)/shard_map/pallas_call | solution.py:408
  44.4 3.4 %all-to-all-start.1 = ((bf16[8,24,728]{2,1,0:T(8,128)(2,1)}), bf16[8,24,728]{2,1,0:T(8,128)(2,1)S(1)}, u32[]{:S(2)}, u32[]{:S(2)}) async-start(bf16[8,24,728]{2,1,0:T(8,128)(2,1)} %shard_map.137), calls=%async_computation.1 | async-start | bytes 589824 | tf_op jit(solution)/shard_map/all_to_all | solution.py:542
  47.8 0.1 collective-permute-start.8
  47.9 0.9 %collective-permute-start.9 = (bf16[48,728]{1,0:T(8,128)(2,1)S(1)}, bf16[48,728]{1,0:T(8,128)(2,1)S(1)}, u32[]{:S(2)}, u32[]{:S(2)}) collective-permute-start(bf16[48,728]{1,0:T(8,128)(2,1)S(1)} %get-tuple-element.47), channel_id=1, source_target_pairs={{0,3},{1,2},{2,1},{3,0},{4,7},{5,6},{6,5},{7,4},{8,11},{9,10},{10,... | collective-permute-start | bytes 209672 | tf_op jit(solution)/shard_map/ppermute | solution.py:544
  48.8 2.5 %shard_map.134 = bf16[6,34944]{1,0:T(8,128)(2,1)} custom-call(bf16[1,6,34944]{2,1,0:T(8,128)(2,1)} %x_ref.5, f32[384,728]{1,0:T(8,128)S(1)} %get-tuple-element.34.proj_ref, f32[8,728]{1,0:T(8,128)S(1)} %get-tuple-element.44.norm_ref, f32[728]{0:T(1024)S(1)} %copy-done.2, f32[728]{0:T(1024)S(1)} %copy-done.3), custom_call_target="tpu_custom_call" | custom-call | tf_op jit(solution)/shard_map/pallas_call | solution.py:408
  51.3 0.6 %collective-permute-done.9.two_ref = bf16[48,728]{1,0:T(8,128)(2,1)S(1)} collective-permute-done((bf16[48,728]{1,0:T(8,128)(2,1)S(1)}, bf16[48,728]{1,0:T(8,128)(2,1)S(1)}, u32[]{:S(2)}, u32[]{:S(2)}) %collective-permute-start.9) | collective-permute-done | bytes 69920 | tf_op jit(solution)/shard_map/ppermute | solution.py:544
  52.0 3.6 %shard_map.135 = bf16[6,34944]{1,0:T(8,128)(2,1)} custom-call(s32[1]{0:T(128)} %bitcast.where_ref, f32[3]{0:T(128)} %class_ref.3, bf16[1,6,34944]{2,1,0:T(8,128)(2,1)} %x_ref.5, bf16[1,6,34944]{2,1,0:T(8,128)(2,1)} %u_ref.3, s32[6,1,48]{2,1,0:T(1,128)} %bitcast.10, f32[48,8,728]{2,1,0:T(8,128)} %get-tuple-element.45.depth_grad_ref, ...), custom_call_target="tpu_custom_call" | custom-call | tf_op jit(solution)/shard_map/pallas_call | solution.py:408
  55.6 0.8 %all-to-all-done.1.refs_0_ = bf16[8,24,728]{2,1,0:T(8,128)(2,1)S(1)} async-done(((bf16[8,24,728]{2,1,0:T(8,128)(2,1)}), bf16[8,24,728]{2,1,0:T(8,128)(2,1)S(1)}, u32[]{:S(2)}, u32[]{:S(2)}) %all-to-all-start.1) | async-done | bytes 279584 | tf_op jit(solution)/shard_map/all_to_all | solution.py:542
  56.4 0.9 %shard_map.138 = (f32[182,728]{1,0:T(8,128)}, f32[9,182]{1,0:T(8,128)}, f32[182]{0:T(256)}, f32[182]{0:T(256)}) custom-call(bf16[8,24,728]{2,1,0:T(8,128)(2,1)S(1)} %all-to-all-done.1.refs_0_), custom_call_target="tpu_custom_call" | custom-call | tf_op jit(solution)/shard_map/pallas_call | solution.py:408
  (16 shorter events, 0.1 us)
Async XLA Ops:
  0.6 7.6 %copy-start.1 = (bf16[9,728]{1,0:T(8,128)(2,1)S(1)}, bf16[9,728]{1,0:T(8,128)(2,1)}, u32[]{:S(2)}) copy-start(bf16[9,728]{1,0:T(8,128)(2,1)} %kernel_ref.5) | copy-start | bytes 39316
  0.6 7.6 %copy-start = (bf16[728,728]{1,0:T(8,128)(2,1)S(1)}, bf16[728,728]{1,0:T(8,128)(2,1)}, u32[]{:S(2)}) copy-start(bf16[728,728]{1,0:T(8,128)(2,1)} %point_ref.3) | copy-start | bytes 3179908
  0.7 7.5 %collective-permute-start = (bf16[1,6,34944]{2,1,0:T(8,128)(2,1)}, bf16[1,6,34944]{2,1,0:T(8,128)(2,1)S(1)}, u32[]{:S(2)}, u32[]{:S(2)}) collective-permute-start(bf16[1,6,34944]{2,1,0:T(8,128)(2,1)} %x_ref.5), channel_id=1, source_target_pairs={{0,1},{1,0},{2,3},{3,2},{4,5},{5,4},{6,7},{7,6},{8,9},{9,8},{10,11... | collective-permute-start | bytes 1257992 | tf_op jit(solution)/shard_map/ppermute | solution.py:447
  2.9 5.3 %collective-permute-start.1 = (bf16[273,128]{1,0:T(8,128)(2,1)S(1)}, bf16[273,128]{1,0:T(8,128)(2,1)S(1)}, u32[]{:S(2)}, u32[]{:S(2)}) collective-permute-start(bf16[273,128]{1,0:T(8,128)(2,1)S(1)} %bitcast.8), channel_id=1, source_target_pairs={{0,3},{1,2},{2,1},{3,0},{4,7},{5,6},{6,5},{7,4},{8,11},{9,10},{10,... | collective-permute-start | bytes 209672 | tf_op jit(solution)/shard_map/ppermute | solution.py:449
  8.2 7.2 %copy-start.2 = (f32[728]{0:T(1024)S(1)}, f32[728]{0:T(1024)}, u32[]{:S(2)}) copy-start(f32[728]{0:T(1024)} %gain_ref.3) | copy-start | bytes 8740
  10.1 5.4 %collective-permute-start.2 = (bf16[384,768]{1,0:T(8,128)(2,1)S(1)}, bf16[384,768]{1,0:T(8,128)(2,1)S(1)}, u32[]{:S(2)}, u32[]{:S(2)}) collective-permute-start(bf16[384,768]{1,0:T(8,128)(2,1)S(1)} %get-tuple-element.35.depth_ref), channel_id=1, source_target_pairs={{0,1},{1,0},{2,3},{3,2},{4,5},{5,4},{6,7},{7,6},{8,9},{9,8},{10,11... | collective-permute-start | bytes 1769480 | tf_op jit(solution)/shard_map/ppermute | solution.py:463
  10.2 3.3 %collective-permute-start.5 = (f32[8,728]{1,0:T(8,128)S(1)}, f32[8,728]{1,0:T(8,128)S(1)}, u32[]{:S(2)}, u32[]{:S(2)}) collective-permute-start(f32[8,728]{1,0:T(8,128)S(1)} %get-tuple-element.36.refs_0_), channel_id=1, source_target_pairs={{0,3},{1,2},{2,1},{3,0},{4,7},{5,6},{6,5},{7,4},{8,11},{9,10},{10,... | collective-permute-start | bytes 69896 | tf_op jit(solution)/shard_map/ppermute | solution.py:467
  11.6 3.8 %collective-permute-start.4 = (f32[8,728]{1,0:T(8,128)S(1)}, f32[8,728]{1,0:T(8,128)S(1)}, u32[]{:S(2)}, u32[]{:S(2)}) collective-permute-start(f32[8,728]{1,0:T(8,128)S(1)} %get-tuple-element.36.refs_0_), channel_id=1, source_target_pairs={{0,2},{1,3},{2,0},{3,1},{4,6},{5,7},{6,4},{7,5},{8,10},{9,11},{10,... | collective-permute-start | bytes 69896 | tf_op jit(solution)/shard_map/ppermute | solution.py:467
  12.3 3.1 %collective-permute-start.3 = (f32[8,728]{1,0:T(8,128)S(1)}, f32[8,728]{1,0:T(8,128)S(1)}, u32[]{:S(2)}, u32[]{:S(2)}) collective-permute-start(f32[8,728]{1,0:T(8,128)S(1)} %get-tuple-element.36.refs_0_), channel_id=1, source_target_pairs={{0,1},{1,0},{2,3},{3,2},{4,5},{5,4},{6,7},{7,6},{8,9},{9,8},{10,11... | collective-permute-start | bytes 69896 | tf_op jit(solution)/shard_map/ppermute | solution.py:467
  15.9 2.1 %collective-permute-start.6 = (bf16[384,768]{1,0:T(8,128)(2,1)S(1)}, bf16[384,768]{1,0:T(8,128)(2,1)S(1)}, u32[]{:S(2)}, u32[]{:S(2)}) collective-permute-start(bf16[384,768]{1,0:T(8,128)(2,1)S(1)} %get-tuple-element.39.full_ref), channel_id=1, source_target_pairs={{0,1},{1,0},{2,3},{3,2},{4,5},{5,4},{6,7},{7,6},{8,9},{9,8},{10,11... | collective-permute-start | bytes 1769480 | tf_op jit(solution)/shard_map/ppermute | solution.py:475
  18.9 9.1 %collective-permute-start.10 = (bf16[182,728]{1,0:T(8,128)(2,1)S(1)}, bf16[182,728]{1,0:T(8,128)(2,1)S(1)}, u32[]{:S(2)}, u32[]{:S(2)}) collective-permute-start(bf16[182,728]{1,0:T(8,128)(2,1)S(1)} %get-tuple-element.49), channel_id=1, source_target_pairs={{0,2},{1,3},{2,0},{3,1},{4,6},{5,7},{6,4},{7,5},{8,10},{9,11},{10,... | collective-permute-start | bytes 794984 | tf_op jit(solution)/shard_map/ppermute | solution.py:505
  22.2 1.3 %collective-permute-start.7 = (f32[16,728]{1,0:T(8,128)S(1)}, f32[16,728]{1,0:T(8,128)S(1)}, u32[]{:S(2)}, u32[]{:S(2)}) collective-permute-start(f32[16,728]{1,0:T(8,128)S(1)} %get-tuple-element.41.taps_ref), channel_id=1, source_target_pairs={{0,1},{1,0},{2,3},{3,2},{4,5},{5,4},{6,7},{7,6},{8,9},{9,8},{10,11... | collective-permute-start | bytes 139784 | tf_op jit(solution)/shard_map/ppermute | solution.py:518
  23.7 4.4 %collective-permute-start.11 = (f32[3,728]{1,0:T(4,128)S(1)}, f32[3,728]{1,0:T(4,128)S(1)}, u32[]{:S(2)}, u32[]{:S(2)}) collective-permute-start(f32[3,728]{1,0:T(4,128)S(1)} %get-tuple-element.51), channel_id=1, source_target_pairs={{0,2},{1,3},{2,0},{3,1},{4,6},{5,7},{6,4},{7,5},{8,10},{9,11},{10,... | collective-permute-start | bytes 26216 | tf_op jit(solution)/shard_map/ppermute | solution.py:522
  28.1 20.8 %copy-start.3 = (f32[728]{0:T(1024)S(1)}, f32[728]{0:T(1024)}, u32[]{:S(2)}) copy-start(f32[728]{0:T(1024)} %shift_ref.1) | copy-start | bytes 8740
  44.4 12.0 %all-to-all-start.1 = ((bf16[8,24,728]{2,1,0:T(8,128)(2,1)}), bf16[8,24,728]{2,1,0:T(8,128)(2,1)S(1)}, u32[]{:S(2)}, u32[]{:S(2)}) async-start(bf16[8,24,728]{2,1,0:T(8,128)(2,1)} %shard_map.137), calls=%async_computation.1 | async-start | bytes 589824 | tf_op jit(solution)/shard_map/all_to_all | solution.py:542
  47.8 3.5 %collective-permute-start.8 = (bf16[48,728]{1,0:T(8,128)(2,1)S(1)}, bf16[48,728]{1,0:T(8,128)(2,1)S(1)}, u32[]{:S(2)}, u32[]{:S(2)}) collective-permute-start(bf16[48,728]{1,0:T(8,128)(2,1)S(1)} %get-tuple-element.46), channel_id=1, source_target_pairs={{0,1},{1,0},{2,3},{3,2},{4,5},{5,4},{6,7},{7,6},{8,9},{9,8},{10,11... | collective-permute-start | bytes 209672 | tf_op jit(solution)/shard_map/ppermute | solution.py:543
  47.9 4.1 %collective-permute-start.9 = (bf16[48,728]{1,0:T(8,128)(2,1)S(1)}, bf16[48,728]{1,0:T(8,128)(2,1)S(1)}, u32[]{:S(2)}, u32[]{:S(2)}) collective-permute-start(bf16[48,728]{1,0:T(8,128)(2,1)S(1)} %get-tuple-element.47), channel_id=1, source_target_pairs={{0,3},{1,2},{2,1},{3,0},{4,7},{5,6},{6,5},{7,4},{8,11},{9,10},{10,... | collective-permute-start | bytes 209672 | tf_op jit(solution)/shard_map/ppermute | solution.py:544

commit v3 on v2

--- a/solution.py
+++ b/solution.py
@@ -157,7 +157,7 @@
     return values[0]
 
 
-def cotangent_kernel(pieces, rows, proj_ref, grad_ref, gain_ref, _, *refs):
+def cotangent_kernel(pieces, rows, proj_ref, grad_ref, gain_ref, *refs):
     stats_refs, (full_ref, norm_ref) = refs[:-2], refs[-2:]
     cols, sub, channels = grad_ref.shape
     local = rows * cols
@@ -445,7 +445,7 @@
     class_buf = pltpu.SMEM(class_weights.shape, F32)
 
     one = lax.ppermute(inputs, "slab", near)
-    edge = jnp.where(even, image[0], image[rows - 1])
+    edge = lax.dynamic_slice_in_dim(image, jnp.where(even, 0, rows - 1), 1, 0)[0]
     two = lax.ppermute(jnp.pad(edge, (0, -flat % LANES)).reshape(-1, LANES), "slab", far)
     own, part, grad_out = call(
         prepare_kernel,
@@ -469,7 +469,7 @@
         all_stats = [lax.all_gather(stats, "slab", axis=0, tiled=True)]
     full, norm = call(
         functools.partial(cotangent_kernel, pieces, rows),
-        [("v", projected), ("v", grad_out), ("v", gain), ("o", other_depth), *(("v", part) for part in all_stats)],
+        [("v", projected), ("v", grad_out), ("v", gain), *(("v", part) for part in all_stats)],
         [("v", (pixels, padded), BF16), ("v", (SUB, channels), F32)],
     )
     theirs = lax.ppermute(full, "slab", near)
@@ -529,6 +529,7 @@
         [("v", (rows, flat), BF16)],
         [flat_buf, pltpu.VMEM((pixels, channels), F32), flat_f32, DMA((2,))],
     )
+    stay, block_out = lax.optimization_barrier((stay, block_out))
     piece = -(-(share + 2 * lines) // copies)
     total = piece * copies
     (packed,) = call(

time: 57.7 us -> 57.3 us (level)
  other arithmetic: 1.71 us -> 0 us
  local copies, waits for them, and re-layouts: 0.02 us -> 1.49 us
    ppermute x1, waiting for transfers between devices: 3.04 us -> 0.56 us  [local(): leave = lax.ppermute(leave, 'slab', across)]
    ppermute x1, waiting for transfers between devices: 0.65 us -> 2.81 us  [local(): halo_two = lax.ppermute(edge_two, 'slab', far)]
    select_n x1 -> x0, other arithmetic: 1.71 us -> none  [local(): edge = jnp.where(even, image[0], image[rows - 1])]
    dynamic_slice x0 -> x1, local copies, waits for them, and re-layouts: none -> 1.47 us  [local(): lax.dynamic_slice_in_dim(image, jnp.where(even, 0, rows - 1), 1, 0)[0]]
  transfers between devices with their start and end apart: 13 -> 13, of which waited for: 7 -> 8; matrix products, arithmetic and copies ran while one was open for 3% -> 3% of each run, Pallas kernels for 21% -> 22%
where the time goes in v3:
time: 57.3 us; the launch traced here: 57 us
  Pallas kernels  17.1 us (30%)
  blocking collectives  15.5 us (27%)
  starting transfers between devices  12.2 us (21%)
  waiting for transfers between devices  9.87 us (17%)
  local copies, waits for them, and re-layouts  1.49 us (3%)
  between operations  0.8 us (1%)
    pallas_call x12, Pallas kernels, call(): pl.pallas_call(body, out_shape=[pltpu.HBM(shape, dtype) if s == 'a' else...  17.1 us
    all_to_all x1, blocking collectives, local(): landed = lax.all_to_all(packed, 'dp', 0, 0)  15.5 us
    all_to_all x1, starting transfers between devices, local(): gathered = lax.all_to_all(summed, 'dp', 0, 0)  3.42 us
    ppermute x3, waiting for transfers between devices, local(): lax.ppermute(stats, 'slab', pairs)  2.91 us
    ppermute x1, waiting for transfers between devices, local(): halo_two = lax.ppermute(edge_two, 'slab', far)  2.81 us
    ppermute x1, starting transfers between devices, local(): lax.ppermute(jnp.pad(edge, (0, -flat % LANES)).reshape(-1, LANES), 'slab'...  2.72 us
    ppermute x3, starting transfers between devices, local(): lax.ppermute(stats, 'slab', pairs)  1.94 us
    ppermute x1, starting transfers between devices, local(): leave = lax.ppermute(leave, 'slab', across)  1.65 us
  transfers between devices with their start and end apart: 13, of which 8 were waited for; matrix products, arithmetic and copies ran while one was open for 3% of the time, Pallas kernels for 22%

profile of v3, /device:TPU:0, one launch (start us, length us, event | category | flops | bytes accessed | tf_op | source)
XLA Modules:
  0.0 57.0 jit_solution(5453302045275294272)
XLA Ops:
  0.7 0.5 collective-permute-start
  1.2 1.5 %dynamic-slice_reduce_fusion = bf16[34944]{0:T(1024)(128)(2,1)S(1)} fusion(bf16[1,6,34944]{2,1,0:T(8,128)(2,1)} %x_ref.5, s32[]{:T(128)S(6)} %select_n.13), kind=kLoop, calls=%fused_computation | loop fusion | bytes 139780 | tf_op jit(solution)/shard_map/dynamic_slice | solution.py:448
  2.6 2.7 %collective-permute-start.1 = (bf16[273,128]{1,0:T(8,128)(2,1)S(1)}, bf16[273,128]{1,0:T(8,128)(2,1)S(1)}, u32[]{:S(2)}, u32[]{:S(2)}) collective-permute-start(bf16[273,128]{1,0:T(8,128)(2,1)S(1)} %bitcast.8), channel_id=1, source_target_pairs={{0,3},{1,2},{2,1},{3,0},{4,7},{5,6},{6,5},{7,4},{8,11},{9,10},{10,... | collective-permute-start | bytes 209672 | tf_op jit(solution)/shard_map/ppermute | solution.py:449
  5.4 2.6 %shard_map.127 = (f32[48,8,728]{2,1,0:T(8,128)S(1)}, f32[48,8,728]{2,1,0:T(8,128)S(1)}, f32[48,8,728]{2,1,0:T(8,128)S(1)}) custom-call(f32[3]{0:T(128)} %class_ref.3, bf16[1,6,34944]{2,1,0:T(8,128)(2,1)} %x_ref.5, bf16[1,6,34944]{2,1,0:T(8,128)(2,1)} %u_ref.3, s32[6,1,48]{2,1,0:T(1,128)} %bitcast.9, bf16[9,728]{1,0:T(8,128)(2,1)} %kernel_ref.5), custom_call_target="tpu_custom_call" | custom-call | tf_op jit(solution)/shard_map/pallas_call | solution.py:408
  8.0 1.9 %shard_map.128 = (bf16[384,768]{1,0:T(8,128)(2,1)S(1)}, f32[384,728]{1,0:T(8,128)S(1)}, f32[48,8,728]{2,1,0:T(8,128)S(1)}, f32[8,728]{1,0:T(8,128)S(1)}) custom-call(s32[1]{0:T(128)} %bitcast.where_ref, f32[48,8,728]{2,1,0:T(8,128)S(1)} %get-tuple-element.33.part_ref, f32[48,8,728]{2,1,0:T(8,128)S(1)} %get-tuple-element.34.own_ref, ...), custom_call_target="tpu_custom_call" | custom-call | tf_op jit(solution)/shard_map/pallas_call | solution.py:408
  9.9 1.4 %collective-permute-start.4 = (f32[8,728]{1,0:T(8,128)S(1)}, f32[8,728]{1,0:T(8,128)S(1)}, u32[]{:S(2)}, u32[]{:S(2)}) collective-permute-start(f32[8,728]{1,0:T(8,128)S(1)} %get-tuple-element.37.refs_0_), channel_id=1, source_target_pairs={{0,3},{1,2},{2,1},{3,0},{4,7},{5,6},{6,5},{7,4},{8,11},{9,10},{10,... | collective-permute-start | bytes 69896 | tf_op jit(solution)/shard_map/ppermute | solution.py:467
  11.2 0.4 collective-permute-start.3
  11.7 0.2 collective-permute-start.2
  11.8 0.3 collective-permute-start.6
  12.2 1.0 %collective-permute-done.4.refs_3_ = f32[8,728]{1,0:T(8,128)S(1)} collective-permute-done((f32[8,728]{1,0:T(8,128)S(1)}, f32[8,728]{1,0:T(8,128)S(1)}, u32[]{:S(2)}, u32[]{:S(2)}) %collective-permute-start.4) | collective-permute-done | bytes 23328 | tf_op jit(solution)/shard_map/ppermute | solution.py:467
  13.2 1.9 %collective-permute-done.3.refs_2_ = f32[8,728]{1,0:T(8,128)S(1)} collective-permute-done((f32[8,728]{1,0:T(8,128)S(1)}, f32[8,728]{1,0:T(8,128)S(1)}, u32[]{:S(2)}, u32[]{:S(2)}) %collective-permute-start.3) | collective-permute-done | bytes 23328 | tf_op jit(solution)/shard_map/ppermute | solution.py:467
  15.1 0.5 shard_map.129
  15.6 0.8 %shard_map.130.own_ref = f32[728,728]{1,0:T(8,128)S(1)} custom-call(bf16[384,768]{1,0:T(8,128)(2,1)S(1)} %get-tuple-element.41.full_ref, bf16[384,768]{1,0:T(8,128)(2,1)S(1)} %get-tuple-element.39.depth_ref), custom_call_target="tpu_custom_call" | custom-call | tf_op jit(solution)/shard_map/pallas_call | solution.py:408
  16.4 1.2 %collective-permute-done.5.full_ref = bf16[384,768]{1,0:T(8,128)(2,1)S(1)} collective-permute-done((bf16[384,768]{1,0:T(8,128)(2,1)S(1)}, bf16[384,768]{1,0:T(8,128)(2,1)S(1)}, u32[]{:S(2)}, u32[]{:S(2)}) %collective-permute-start.5) | collective-permute-done | bytes 589856 | tf_op jit(solution)/shard_map/ppermute | solution.py:475
  17.6 1.0 %shard_map.131 = (f32[182,728]{1,0:T(8,128)S(1)}, bf16[182,728]{1,0:T(8,128)(2,1)S(1)}) custom-call(s32[1]{0:T(128)} %bitcast.where_ref, bf16[384,768]{1,0:T(8,128)(2,1)S(1)} %collective-permute-done.5.full_ref, bf16[384,768]{1,0:T(8,128)(2,1)S(1)} %collective-permute-done.6.depth_ref, f32[728,728]{1,0:T(8,128)S(1)} %shard_map.130.own_ref), custom_call_target="tpu_custom_call" | custom-call | tf_op jit(solution)/shard_map/pallas_call | solution.py:408
  18.6 0.5 collective-permute-start.10
  19.1 2.5 %shard_map.132 = (f32[48,8,728]{2,1,0:T(8,128)}, f32[16,728]{1,0:T(8,128)S(1)}, bf16[48,728]{1,0:T(8,128)(2,1)S(1)}, bf16[48,728]{1,0:T(8,128)(2,1)S(1)}) custom-call(s32[1]{0:T(128)} %bitcast.where_ref, bf16[384,768]{1,0:T(8,128)(2,1)S(1)} %get-tuple-element.41.full_ref, bf16[728,728]{1,0:T(8,128)(2,1)S(1)} %copy-done, ...), custom_call_target="tpu_custom_call" | custom-call | tf_op jit(solution)/shard_map/pallas_call | solution.py:408
  21.7 1.2 %collective-permute-done.7.other_ref = f32[16,728]{1,0:T(8,128)S(1)} collective-permute-done((f32[16,728]{1,0:T(8,128)S(1)}, f32[16,728]{1,0:T(8,128)S(1)}, u32[]{:S(2)}, u32[]{:S(2)}) %collective-permute-start.7) | collective-permute-done | bytes 46624 | tf_op jit(solution)/shard_map/ppermute | solution.py:518
  22.9 0.1 shard_map.133
  23.0 1.6 %collective-permute-start.11 = (f32[3,728]{1,0:T(4,128)S(1)}, f32[3,728]{1,0:T(4,128)S(1)}, u32[]{:S(2)}, u32[]{:S(2)}) collective-permute-start(f32[3,728]{1,0:T(4,128)S(1)} %get-tuple-element.55), channel_id=1, source_target_pairs={{0,2},{1,3},{2,0},{3,1},{4,6},{5,7},{6,4},{7,5},{8,10},{9,11},{10,... | collective-permute-start | bytes 26216 | tf_op jit(solution)/shard_map/ppermute | solution.py:522
  24.7 2.5 %shard_map.134 = bf16[6,34944]{1,0:T(8,128)(2,1)} custom-call(bf16[1,6,34944]{2,1,0:T(8,128)(2,1)} %x_ref.5, f32[384,728]{1,0:T(8,128)S(1)} %get-tuple-element.36.proj_ref, f32[8,728]{1,0:T(8,128)S(1)} %get-tuple-element.47.norm_ref, f32[728]{0:T(1024)S(1)} %copy-done.2, f32[728]{0:T(1024)S(1)} %copy-done.3), custom_call_target="tpu_custom_call" | custom-call | tf_op jit(solution)/shard_map/pallas_call | solution.py:408
  27.2 0.6 collective-permute-done.11.other_ref
  27.7 0.1 shard_map.136
  27.8 15.5 %all_to_all.10.in_ref = bf16[8,24,728]{2,1,0:T(8,128)(2,1)S(1)} all-to-all(bf16[8,24,728]{2,1,0:T(8,128)(2,1)S(1)} %shard_map.136), channel_id=1, replica_groups=mesh['dp'=8,'slab'=4] {'dp'}, dimensions={0} | all-to-all | bytes 559104 | tf_op jit(solution)/shard_map/all_to_all | solution.py:541
  43.3 0.8 %shard_map.137 = bf16[8,24,728]{2,1,0:T(8,128)(2,1)} custom-call(bf16[8,24,728]{2,1,0:T(8,128)(2,1)S(1)} %all_to_all.10.in_ref), custom_call_target="tpu_custom_call" | custom-call | tf_op jit(solution)/shard_map/pallas_call | solution.py:408
  44.1 3.4 %all-to-all-start.1 = ((bf16[8,24,728]{2,1,0:T(8,128)(2,1)}), bf16[8,24,728]{2,1,0:T(8,128)(2,1)S(1)}, u32[]{:S(2)}, u32[]{:S(2)}) async-start(bf16[8,24,728]{2,1,0:T(8,128)(2,1)} %shard_map.137), calls=%async_computation.1 | async-start | bytes 589824 | tf_op jit(solution)/shard_map/all_to_all | solution.py:543
  47.6 0.9 %collective-permute-start.9 = (bf16[48,728]{1,0:T(8,128)(2,1)S(1)}, bf16[48,728]{1,0:T(8,128)(2,1)S(1)}, u32[]{:S(2)}, u32[]{:S(2)}) collective-permute-start(bf16[48,728]{1,0:T(8,128)(2,1)S(1)} %get-tuple-element.51), channel_id=1, source_target_pairs={{0,3},{1,2},{2,1},{3,0},{4,7},{5,6},{6,5},{7,4},{8,11},{9,10},{10,... | collective-permute-start | bytes 209672 | tf_op jit(solution)/shard_map/ppermute | solution.py:545
  48.5 0.3 collective-permute-done.8.one_ref
  48.8 2.8 %collective-permute-done.9.two_ref = bf16[48,728]{1,0:T(8,128)(2,1)S(1)} collective-permute-done((bf16[48,728]{1,0:T(8,128)(2,1)S(1)}, bf16[48,728]{1,0:T(8,128)(2,1)S(1)}, u32[]{:S(2)}, u32[]{:S(2)}) %collective-permute-start.9) | collective-permute-done | bytes 69920 | tf_op jit(solution)/shard_map/ppermute | solution.py:545
  51.6 3.6 %shard_map.135 = bf16[6,34944]{1,0:T(8,128)(2,1)} custom-call(s32[1]{0:T(128)} %bitcast.where_ref, f32[3]{0:T(128)} %class_ref.3, bf16[1,6,34944]{2,1,0:T(8,128)(2,1)} %x_ref.5, bf16[1,6,34944]{2,1,0:T(8,128)(2,1)} %u_ref.3, s32[6,1,48]{2,1,0:T(1,128)} %bitcast.10, f32[48,8,728]{2,1,0:T(8,128)} %get-tuple-element.49.depth_grad_ref, ...), custom_call_target="tpu_custom_call" | custom-call | tf_op jit(solution)/shard_map/pallas_call | solution.py:408
  55.2 0.8 %all-to-all-done.1.refs_0_ = bf16[8,24,728]{2,1,0:T(8,128)(2,1)S(1)} async-done(((bf16[8,24,728]{2,1,0:T(8,128)(2,1)}), bf16[8,24,728]{2,1,0:T(8,128)(2,1)S(1)}, u32[]{:S(2)}, u32[]{:S(2)}) %all-to-all-start.1) | async-done | bytes 279584 | tf_op jit(solution)/shard_map/all_to_all | solution.py:543
  56.1 0.9 %shard_map.138 = (f32[182,728]{1,0:T(8,128)}, f32[9,182]{1,0:T(8,128)}, f32[182]{0:T(256)}, f32[182]{0:T(256)}) custom-call(bf16[8,24,728]{2,1,0:T(8,128)(2,1)S(1)} %all-to-all-done.1.refs_0_), custom_call_target="tpu_custom_call" | custom-call | tf_op jit(solution)/shard_map/pallas_call | solution.py:408
  (16 shorter events, 0.2 us)
Async XLA Ops:
  0.6 7.3 %copy-start.1 = (bf16[9,728]{1,0:T(8,128)(2,1)S(1)}, bf16[9,728]{1,0:T(8,128)(2,1)}, u32[]{:S(2)}) copy-start(bf16[9,728]{1,0:T(8,128)(2,1)} %kernel_ref.5) | copy-start | bytes 39316
  0.6 7.3 %copy-start = (bf16[728,728]{1,0:T(8,128)(2,1)S(1)}, bf16[728,728]{1,0:T(8,128)(2,1)}, u32[]{:S(2)}) copy-start(bf16[728,728]{1,0:T(8,128)(2,1)} %point_ref.3) | copy-start | bytes 3179908
  0.7 7.3 %collective-permute-start = (bf16[1,6,34944]{2,1,0:T(8,128)(2,1)}, bf16[1,6,34944]{2,1,0:T(8,128)(2,1)S(1)}, u32[]{:S(2)}, u32[]{:S(2)}) collective-permute-start(bf16[1,6,34944]{2,1,0:T(8,128)(2,1)} %x_ref.5), channel_id=1, source_target_pairs={{0,1},{1,0},{2,3},{3,2},{4,5},{5,4},{6,7},{7,6},{8,9},{9,8},{10,11... | collective-permute-start | bytes 1257992 | tf_op jit(solution)/shard_map/ppermute | solution.py:447
  2.6 5.3 %collective-permute-start.1 = (bf16[273,128]{1,0:T(8,128)(2,1)S(1)}, bf16[273,128]{1,0:T(8,128)(2,1)S(1)}, u32[]{:S(2)}, u32[]{:S(2)}) collective-permute-start(bf16[273,128]{1,0:T(8,128)(2,1)S(1)} %bitcast.8), channel_id=1, source_target_pairs={{0,3},{1,2},{2,1},{3,0},{4,7},{5,6},{6,5},{7,4},{8,11},{9,10},{10,... | collective-permute-start | bytes 209672 | tf_op jit(solution)/shard_map/ppermute | solution.py:449
  8.0 7.1 %copy-start.2 = (f32[728]{0:T(1024)S(1)}, f32[728]{0:T(1024)}, u32[]{:S(2)}) copy-start(f32[728]{0:T(1024)} %gain_ref.3) | copy-start | bytes 8740
  9.9 3.3 %collective-permute-start.4 = (f32[8,728]{1,0:T(8,128)S(1)}, f32[8,728]{1,0:T(8,128)S(1)}, u32[]{:S(2)}, u32[]{:S(2)}) collective-permute-start(f32[8,728]{1,0:T(8,128)S(1)} %get-tuple-element.37.refs_0_), channel_id=1, source_target_pairs={{0,3},{1,2},{2,1},{3,0},{4,7},{5,6},{6,5},{7,4},{8,11},{9,10},{10,... | collective-permute-start | bytes 69896 | tf_op jit(solution)/shard_map/ppermute | solution.py:467
  11.2 3.8 %collective-permute-start.3 = (f32[8,728]{1,0:T(8,128)S(1)}, f32[8,728]{1,0:T(8,128)S(1)}, u32[]{:S(2)}, u32[]{:S(2)}) collective-permute-start(f32[8,728]{1,0:T(8,128)S(1)} %get-tuple-element.37.refs_0_), channel_id=1, source_target_pairs={{0,2},{1,3},{2,0},{3,1},{4,6},{5,7},{6,4},{7,5},{8,10},{9,11},{10,... | collective-permute-start | bytes 69896 | tf_op jit(solution)/shard_map/ppermute | solution.py:467
  11.7 3.4 %collective-permute-start.2 = (f32[8,728]{1,0:T(8,128)S(1)}, f32[8,728]{1,0:T(8,128)S(1)}, u32[]{:S(2)}, u32[]{:S(2)}) collective-permute-start(f32[8,728]{1,0:T(8,128)S(1)} %get-tuple-element.37.refs_0_), channel_id=1, source_target_pairs={{0,1},{1,0},{2,3},{3,2},{4,5},{5,4},{6,7},{7,6},{8,9},{9,8},{10,11... | collective-permute-start | bytes 69896 | tf_op jit(solution)/shard_map/ppermute | solution.py:467
  11.8 4.6 %collective-permute-start.6 = (bf16[384,768]{1,0:T(8,128)(2,1)S(1)}, bf16[384,768]{1,0:T(8,128)(2,1)S(1)}, u32[]{:S(2)}, u32[]{:S(2)}) collective-permute-start(bf16[384,768]{1,0:T(8,128)(2,1)S(1)} %get-tuple-element.39.depth_ref), channel_id=1, source_target_pairs={{0,1},{1,0},{2,3},{3,2},{4,5},{5,4},{6,7},{7,6},{8,9},{9,8},{10,11... | collective-permute-start | bytes 1769480 | tf_op jit(solution)/shard_map/ppermute | solution.py:463
  15.5 2.1 %collective-permute-start.5 = (bf16[384,768]{1,0:T(8,128)(2,1)S(1)}, bf16[384,768]{1,0:T(8,128)(2,1)S(1)}, u32[]{:S(2)}, u32[]{:S(2)}) collective-permute-start(bf16[384,768]{1,0:T(8,128)(2,1)S(1)} %get-tuple-element.41.full_ref), channel_id=1, source_target_pairs={{0,1},{1,0},{2,3},{3,2},{4,5},{5,4},{6,7},{7,6},{8,9},{9,8},{10,11... | collective-permute-start | bytes 1769480 | tf_op jit(solution)/shard_map/ppermute | solution.py:475
  18.6 9.1 %collective-permute-start.10 = (bf16[182,728]{1,0:T(8,128)(2,1)S(1)}, bf16[182,728]{1,0:T(8,128)(2,1)S(1)}, u32[]{:S(2)}, u32[]{:S(2)}) collective-permute-start(bf16[182,728]{1,0:T(8,128)(2,1)S(1)} %get-tuple-element.53), channel_id=1, source_target_pairs={{0,2},{1,3},{2,0},{3,1},{4,6},{5,7},{6,4},{7,5},{8,10},{9,11},{10,... | collective-permute-start | bytes 794984 | tf_op jit(solution)/shard_map/ppermute | solution.py:505
  19.1 5.6 %copy-start.3 = (f32[728]{0:T(1024)S(1)}, f32[728]{0:T(1024)}, u32[]{:S(2)}) copy-start(f32[728]{0:T(1024)} %shift_ref.1) | copy-start | bytes 8740
  21.6 1.3 %collective-permute-start.7 = (f32[16,728]{1,0:T(8,128)S(1)}, f32[16,728]{1,0:T(8,128)S(1)}, u32[]{:S(2)}, u32[]{:S(2)}) collective-permute-start(f32[16,728]{1,0:T(8,128)S(1)} %get-tuple-element.43.taps_ref), channel_id=1, source_target_pairs={{0,1},{1,0},{2,3},{3,2},{4,5},{5,4},{6,7},{7,6},{8,9},{9,8},{10,11... | collective-permute-start | bytes 139784 | tf_op jit(solution)/shard_map/ppermute | solution.py:518
  23.0 4.7 %collective-permute-start.11 = (f32[3,728]{1,0:T(4,128)S(1)}, f32[3,728]{1,0:T(4,128)S(1)}, u32[]{:S(2)}, u32[]{:S(2)}) collective-permute-start(f32[3,728]{1,0:T(4,128)S(1)} %get-tuple-element.55), channel_id=1, source_target_pairs={{0,2},{1,3},{2,0},{3,1},{4,6},{5,7},{6,4},{7,5},{8,10},{9,11},{10,... | collective-permute-start | bytes 26216 | tf_op jit(solution)/shard_map/ppermute | solution.py:522
  44.1 12.0 %all-to-all-start.1 = ((bf16[8,24,728]{2,1,0:T(8,128)(2,1)}), bf16[8,24,728]{2,1,0:T(8,128)(2,1)S(1)}, u32[]{:S(2)}, u32[]{:S(2)}) async-start(bf16[8,24,728]{2,1,0:T(8,128)(2,1)} %shard_map.137), calls=%async_computation.1 | async-start | bytes 589824 | tf_op jit(solution)/shard_map/all_to_all | solution.py:543
  47.5 1.3 %collective-permute-start.8 = (bf16[48,728]{1,0:T(8,128)(2,1)S(1)}, bf16[48,728]{1,0:T(8,128)(2,1)S(1)}, u32[]{:S(2)}, u32[]{:S(2)}) collective-permute-start(bf16[48,728]{1,0:T(8,128)(2,1)S(1)} %get-tuple-element.50), channel_id=1, source_target_pairs={{0,1},{1,0},{2,3},{3,2},{4,5},{5,4},{6,7},{7,6},{8,9},{9,8},{10,11... | collective-permute-start | bytes 209672 | tf_op jit(solution)/shard_map/ppermute | solution.py:544
  47.6 4.1 %collective-permute-start.9 = (bf16[48,728]{1,0:T(8,128)(2,1)S(1)}, bf16[48,728]{1,0:T(8,128)(2,1)S(1)}, u32[]{:S(2)}, u32[]{:S(2)}) collective-permute-start(bf16[48,728]{1,0:T(8,128)(2,1)S(1)} %get-tuple-element.51), channel_id=1, source_target_pairs={{0,3},{1,2},{2,1},{3,0},{4,7},{5,6},{6,5},{7,4},{8,11},{9,10},{10,... | collective-permute-start | bytes 209672 | tf_op jit(solution)/shard_map/ppermute | solution.py:545

commit v4 on v3

--- a/solution.py
+++ b/solution.py
@@ -316,6 +316,10 @@
         out_ref[k] = total
 
 
+def scaled(values, batch):
+    return values * (1.0 / batch) if batch & (batch - 1) == 0 else values / batch
+
+
 def unpack_kernel(pieces, batch, *refs):
     ins, (point_ref, tap_ref, gain_ref, shift_ref, flat_ref) = refs[:-5], refs[-5:]
     share = point_ref.shape[0]
@@ -323,7 +327,7 @@
     for in_ref in ins:
         copies, piece, _ = in_ref.shape
         for k in range(copies):
-            flat_ref[start : start + piece, :] = in_ref[k].astype(F32) / batch
+            flat_ref[start : start + piece, :] = scaled(in_ref[k].astype(F32), batch)
             start += piece
     point_ref[...] = flat_ref[:share, :]
     lines = -(-11 // pieces)

time: 57.3 us -> 57.3 us (level)
  no operation moved by 1% of the time
where the time goes in v4:
time: 57.3 us; the launch traced here: 57 us
  Pallas kernels  17.1 us (30%)
  blocking collectives  15.5 us (27%)
  starting transfers between devices  12.2 us (21%)
  waiting for transfers between devices  9.87 us (17%)
  local copies, waits for them, and re-layouts  1.49 us (3%)
  between operations  0.8 us (1%)
    pallas_call x12, Pallas kernels, call(): pl.pallas_call(body, out_shape=[pltpu.HBM(shape, dtype) if s == 'a' else...  17.1 us
    all_to_all x1, blocking collectives, local(): landed = lax.all_to_all(packed, 'dp', 0, 0)  15.5 us
    all_to_all x1, starting transfers between devices, local(): gathered = lax.all_to_all(summed, 'dp', 0, 0)  3.42 us
    ppermute x3, waiting for transfers between devices, local(): lax.ppermute(stats, 'slab', pairs)  2.91 us
    ppermute x1, waiting for transfers between devices, local(): halo_two = lax.ppermute(edge_two, 'slab', far)  2.81 us
    ppermute x1, starting transfers between devices, local(): lax.ppermute(jnp.pad(edge, (0, -flat % LANES)).reshape(-1, LANES), 'slab'...  2.72 us
    ppermute x3, starting transfers between devices, local(): lax.ppermute(stats, 'slab', pairs)  1.94 us
    ppermute x1, starting transfers between devices, local(): leave = lax.ppermute(leave, 'slab', across)  1.65 us
  transfers between devices with their start and end apart: 13, of which 8 were waited for; matrix products, arithmetic and copies ran while one was open for 3% of the time, Pallas kernels for 22%

profile of v4, /device:TPU:0, one launch (start us, length us, event | category | flops | bytes accessed | tf_op | source)
XLA Modules:
  0.0 57.0 jit_solution(5453302045275294272)
XLA Ops:
  0.7 0.5 collective-permute-start
  1.2 1.5 %dynamic-slice_reduce_fusion = bf16[34944]{0:T(1024)(128)(2,1)S(1)} fusion(bf16[1,6,34944]{2,1,0:T(8,128)(2,1)} %x_ref.5, s32[]{:T(128)S(6)} %select_n.13), kind=kLoop, calls=%fused_computation | loop fusion | bytes 139780 | tf_op jit(solution)/shard_map/dynamic_slice | solution.py:452
  2.6 2.7 %collective-permute-start.1 = (bf16[273,128]{1,0:T(8,128)(2,1)S(1)}, bf16[273,128]{1,0:T(8,128)(2,1)S(1)}, u32[]{:S(2)}, u32[]{:S(2)}) collective-permute-start(bf16[273,128]{1,0:T(8,128)(2,1)S(1)} %bitcast.8), channel_id=1, source_target_pairs={{0,3},{1,2},{2,1},{3,0},{4,7},{5,6},{6,5},{7,4},{8,11},{9,10},{10,... | collective-permute-start | bytes 209672 | tf_op jit(solution)/shard_map/ppermute | solution.py:453
  5.4 2.6 %shard_map.127 = (f32[48,8,728]{2,1,0:T(8,128)S(1)}, f32[48,8,728]{2,1,0:T(8,128)S(1)}, f32[48,8,728]{2,1,0:T(8,128)S(1)}) custom-call(f32[3]{0:T(128)} %class_ref.3, bf16[1,6,34944]{2,1,0:T(8,128)(2,1)} %x_ref.5, bf16[1,6,34944]{2,1,0:T(8,128)(2,1)} %u_ref.3, s32[6,1,48]{2,1,0:T(1,128)} %bitcast.9, bf16[9,728]{1,0:T(8,128)(2,1)} %kernel_ref.5), custom_call_target="tpu_custom_call" | custom-call | tf_op jit(solution)/shard_map/pallas_call | solution.py:412
  8.0 1.9 %shard_map.128 = (bf16[384,768]{1,0:T(8,128)(2,1)S(1)}, f32[384,728]{1,0:T(8,128)S(1)}, f32[48,8,728]{2,1,0:T(8,128)S(1)}, f32[8,728]{1,0:T(8,128)S(1)}) custom-call(s32[1]{0:T(128)} %bitcast.where_ref, f32[48,8,728]{2,1,0:T(8,128)S(1)} %get-tuple-element.33.part_ref, f32[48,8,728]{2,1,0:T(8,128)S(1)} %get-tuple-element.34.own_ref, ...), custom_call_target="tpu_custom_call" | custom-call | tf_op jit(solution)/shard_map/pallas_call | solution.py:412
  9.9 1.4 %collective-permute-start.4 = (f32[8,728]{1,0:T(8,128)S(1)}, f32[8,728]{1,0:T(8,128)S(1)}, u32[]{:S(2)}, u32[]{:S(2)}) collective-permute-start(f32[8,728]{1,0:T(8,128)S(1)} %get-tuple-element.37.refs_0_), channel_id=1, source_target_pairs={{0,3},{1,2},{2,1},{3,0},{4,7},{5,6},{6,5},{7,4},{8,11},{9,10},{10,... | collective-permute-start | bytes 69896 | tf_op jit(solution)/shard_map/ppermute | solution.py:471
  11.2 0.4 collective-permute-start.3
  11.7 0.2 collective-permute-start.2
  11.8 0.3 collective-permute-start.6
  12.2 1.0 %collective-permute-done.4.refs_3_ = f32[8,728]{1,0:T(8,128)S(1)} collective-permute-done((f32[8,728]{1,0:T(8,128)S(1)}, f32[8,728]{1,0:T(8,128)S(1)}, u32[]{:S(2)}, u32[]{:S(2)}) %collective-permute-start.4) | collective-permute-done | bytes 23328 | tf_op jit(solution)/shard_map/ppermute | solution.py:471
  13.2 1.9 %collective-permute-done.3.refs_2_ = f32[8,728]{1,0:T(8,128)S(1)} collective-permute-done((f32[8,728]{1,0:T(8,128)S(1)}, f32[8,728]{1,0:T(8,128)S(1)}, u32[]{:S(2)}, u32[]{:S(2)}) %collective-permute-start.3) | collective-permute-done | bytes 23328 | tf_op jit(solution)/shard_map/ppermute | solution.py:471
  15.1 0.5 shard_map.129
  15.6 0.8 %shard_map.130.own_ref = f32[728,728]{1,0:T(8,128)S(1)} custom-call(bf16[384,768]{1,0:T(8,128)(2,1)S(1)} %get-tuple-element.41.full_ref, bf16[384,768]{1,0:T(8,128)(2,1)S(1)} %get-tuple-element.39.depth_ref), custom_call_target="tpu_custom_call" | custom-call | tf_op jit(solution)/shard_map/pallas_call | solution.py:412
  16.4 1.2 %collective-permute-done.5.full_ref = bf16[384,768]{1,0:T(8,128)(2,1)S(1)} collective-permute-done((bf16[384,768]{1,0:T(8,128)(2,1)S(1)}, bf16[384,768]{1,0:T(8,128)(2,1)S(1)}, u32[]{:S(2)}, u32[]{:S(2)}) %collective-permute-start.5) | collective-permute-done | bytes 589856 | tf_op jit(solution)/shard_map/ppermute | solution.py:479
  17.6 1.0 %shard_map.131 = (f32[182,728]{1,0:T(8,128)S(1)}, bf16[182,728]{1,0:T(8,128)(2,1)S(1)}) custom-call(s32[1]{0:T(128)} %bitcast.where_ref, bf16[384,768]{1,0:T(8,128)(2,1)S(1)} %collective-permute-done.5.full_ref, bf16[384,768]{1,0:T(8,128)(2,1)S(1)} %collective-permute-done.6.depth_ref, f32[728,728]{1,0:T(8,128)S(1)} %shard_map.130.own_ref), custom_call_target="tpu_custom_call" | custom-call | tf_op jit(solution)/shard_map/pallas_call | solution.py:412
  18.6 0.5 collective-permute-start.10
  19.1 2.5 %shard_map.132 = (f32[48,8,728]{2,1,0:T(8,128)}, f32[16,728]{1,0:T(8,128)S(1)}, bf16[48,728]{1,0:T(8,128)(2,1)S(1)}, bf16[48,728]{1,0:T(8,128)(2,1)S(1)}) custom-call(s32[1]{0:T(128)} %bitcast.where_ref, bf16[384,768]{1,0:T(8,128)(2,1)S(1)} %get-tuple-element.41.full_ref, bf16[728,728]{1,0:T(8,128)(2,1)S(1)} %copy-done, ...), custom_call_target="tpu_custom_call" | custom-call | tf_op jit(solution)/shard_map/pallas_call | solution.py:412
  21.7 1.2 %collective-permute-done.7.other_ref = f32[16,728]{1,0:T(8,128)S(1)} collective-permute-done((f32[16,728]{1,0:T(8,128)S(1)}, f32[16,728]{1,0:T(8,128)S(1)}, u32[]{:S(2)}, u32[]{:S(2)}) %collective-permute-start.7) | collective-permute-done | bytes 46624 | tf_op jit(solution)/shard_map/ppermute | solution.py:522
  22.9 0.1 shard_map.133
  23.0 1.6 %collective-permute-start.11 = (f32[3,728]{1,0:T(4,128)S(1)}, f32[3,728]{1,0:T(4,128)S(1)}, u32[]{:S(2)}, u32[]{:S(2)}) collective-permute-start(f32[3,728]{1,0:T(4,128)S(1)} %get-tuple-element.55), channel_id=1, source_target_pairs={{0,2},{1,3},{2,0},{3,1},{4,6},{5,7},{6,4},{7,5},{8,10},{9,11},{10,... | collective-permute-start | bytes 26216 | tf_op jit(solution)/shard_map/ppermute | solution.py:526
  24.7 2.5 %shard_map.134 = bf16[6,34944]{1,0:T(8,128)(2,1)} custom-call(bf16[1,6,34944]{2,1,0:T(8,128)(2,1)} %x_ref.5, f32[384,728]{1,0:T(8,128)S(1)} %get-tuple-element.36.proj_ref, f32[8,728]{1,0:T(8,128)S(1)} %get-tuple-element.47.norm_ref, f32[728]{0:T(1024)S(1)} %copy-done.2, f32[728]{0:T(1024)S(1)} %copy-done.3), custom_call_target="tpu_custom_call" | custom-call | tf_op jit(solution)/shard_map/pallas_call | solution.py:412
  27.2 0.6 collective-permute-done.11.other_ref
  27.7 0.1 shard_map.136
  27.8 15.5 %all_to_all.10.in_ref = bf16[8,24,728]{2,1,0:T(8,128)(2,1)S(1)} all-to-all(bf16[8,24,728]{2,1,0:T(8,128)(2,1)S(1)} %shard_map.136), channel_id=1, replica_groups=mesh['dp'=8,'slab'=4] {'dp'}, dimensions={0} | all-to-all | bytes 559104 | tf_op jit(solution)/shard_map/all_to_all | solution.py:545
  43.3 0.8 %shard_map.137 = bf16[8,24,728]{2,1,0:T(8,128)(2,1)} custom-call(bf16[8,24,728]{2,1,0:T(8,128)(2,1)S(1)} %all_to_all.10.in_ref), custom_call_target="tpu_custom_call" | custom-call | tf_op jit(solution)/shard_map/pallas_call | solution.py:412
  44.1 3.4 %all-to-all-start.1 = ((bf16[8,24,728]{2,1,0:T(8,128)(2,1)}), bf16[8,24,728]{2,1,0:T(8,128)(2,1)S(1)}, u32[]{:S(2)}, u32[]{:S(2)}) async-start(bf16[8,24,728]{2,1,0:T(8,128)(2,1)} %shard_map.137), calls=%async_computation.1 | async-start | bytes 589824 | tf_op jit(solution)/shard_map/all_to_all | solution.py:547
  47.6 0.9 %collective-permute-start.9 = (bf16[48,728]{1,0:T(8,128)(2,1)S(1)}, bf16[48,728]{1,0:T(8,128)(2,1)S(1)}, u32[]{:S(2)}, u32[]{:S(2)}) collective-permute-start(bf16[48,728]{1,0:T(8,128)(2,1)S(1)} %get-tuple-element.51), channel_id=1, source_target_pairs={{0,3},{1,2},{2,1},{3,0},{4,7},{5,6},{6,5},{7,4},{8,11},{9,10},{10,... | collective-permute-start | bytes 209672 | tf_op jit(solution)/shard_map/ppermute | solution.py:549
  48.5 0.3 collective-permute-done.8.one_ref
  48.8 2.8 %collective-permute-done.9.two_ref = bf16[48,728]{1,0:T(8,128)(2,1)S(1)} collective-permute-done((bf16[48,728]{1,0:T(8,128)(2,1)S(1)}, bf16[48,728]{1,0:T(8,128)(2,1)S(1)}, u32[]{:S(2)}, u32[]{:S(2)}) %collective-permute-start.9) | collective-permute-done | bytes 69920 | tf_op jit(solution)/shard_map/ppermute | solution.py:549
  51.6 3.6 %shard_map.135 = bf16[6,34944]{1,0:T(8,128)(2,1)} custom-call(s32[1]{0:T(128)} %bitcast.where_ref, f32[3]{0:T(128)} %class_ref.3, bf16[1,6,34944]{2,1,0:T(8,128)(2,1)} %x_ref.5, bf16[1,6,34944]{2,1,0:T(8,128)(2,1)} %u_ref.3, s32[6,1,48]{2,1,0:T(1,128)} %bitcast.10, f32[48,8,728]{2,1,0:T(8,128)} %get-tuple-element.49.depth_grad_ref, ...), custom_call_target="tpu_custom_call" | custom-call | tf_op jit(solution)/shard_map/pallas_call | solution.py:412
  55.2 0.8 %all-to-all-done.1.refs_0_ = bf16[8,24,728]{2,1,0:T(8,128)(2,1)S(1)} async-done(((bf16[8,24,728]{2,1,0:T(8,128)(2,1)}), bf16[8,24,728]{2,1,0:T(8,128)(2,1)S(1)}, u32[]{:S(2)}, u32[]{:S(2)}) %all-to-all-start.1) | async-done | bytes 279584 | tf_op jit(solution)/shard_map/all_to_all | solution.py:547
  56.1 0.9 %shard_map.138 = (f32[182,728]{1,0:T(8,128)}, f32[9,182]{1,0:T(8,128)}, f32[182]{0:T(256)}, f32[182]{0:T(256)}) custom-call(bf16[8,24,728]{2,1,0:T(8,128)(2,1)S(1)} %all-to-all-done.1.refs_0_), custom_call_target="tpu_custom_call" | custom-call | tf_op jit(solution)/shard_map/pallas_call | solution.py:412
  (16 shorter events, 0.2 us)
Async XLA Ops:
  0.6 7.3 %copy-start.1 = (bf16[9,728]{1,0:T(8,128)(2,1)S(1)}, bf16[9,728]{1,0:T(8,128)(2,1)}, u32[]{:S(2)}) copy-start(bf16[9,728]{1,0:T(8,128)(2,1)} %kernel_ref.5) | copy-start | bytes 39316
  0.6 7.3 %copy-start = (bf16[728,728]{1,0:T(8,128)(2,1)S(1)}, bf16[728,728]{1,0:T(8,128)(2,1)}, u32[]{:S(2)}) copy-start(bf16[728,728]{1,0:T(8,128)(2,1)} %point_ref.3) | copy-start | bytes 3179908
  0.7 7.3 %collective-permute-start = (bf16[1,6,34944]{2,1,0:T(8,128)(2,1)}, bf16[1,6,34944]{2,1,0:T(8,128)(2,1)S(1)}, u32[]{:S(2)}, u32[]{:S(2)}) collective-permute-start(bf16[1,6,34944]{2,1,0:T(8,128)(2,1)} %x_ref.5), channel_id=1, source_target_pairs={{0,1},{1,0},{2,3},{3,2},{4,5},{5,4},{6,7},{7,6},{8,9},{9,8},{10,11... | collective-permute-start | bytes 1257992 | tf_op jit(solution)/shard_map/ppermute | solution.py:451
  2.6 5.3 %collective-permute-start.1 = (bf16[273,128]{1,0:T(8,128)(2,1)S(1)}, bf16[273,128]{1,0:T(8,128)(2,1)S(1)}, u32[]{:S(2)}, u32[]{:S(2)}) collective-permute-start(bf16[273,128]{1,0:T(8,128)(2,1)S(1)} %bitcast.8), channel_id=1, source_target_pairs={{0,3},{1,2},{2,1},{3,0},{4,7},{5,6},{6,5},{7,4},{8,11},{9,10},{10,... | collective-permute-start | bytes 209672 | tf_op jit(solution)/shard_map/ppermute | solution.py:453
  8.0 7.1 %copy-start.2 = (f32[728]{0:T(1024)S(1)}, f32[728]{0:T(1024)}, u32[]{:S(2)}) copy-start(f32[728]{0:T(1024)} %gain_ref.3) | copy-start | bytes 8740
  9.9 3.3 %collective-permute-start.4 = (f32[8,728]{1,0:T(8,128)S(1)}, f32[8,728]{1,0:T(8,128)S(1)}, u32[]{:S(2)}, u32[]{:S(2)}) collective-permute-start(f32[8,728]{1,0:T(8,128)S(1)} %get-tuple-element.37.refs_0_), channel_id=1, source_target_pairs={{0,3},{1,2},{2,1},{3,0},{4,7},{5,6},{6,5},{7,4},{8,11},{9,10},{10,... | collective-permute-start | bytes 69896 | tf_op jit(solution)/shard_map/ppermute | solution.py:471
  11.2 3.8 %collective-permute-start.3 = (f32[8,728]{1,0:T(8,128)S(1)}, f32[8,728]{1,0:T(8,128)S(1)}, u32[]{:S(2)}, u32[]{:S(2)}) collective-permute-start(f32[8,728]{1,0:T(8,128)S(1)} %get-tuple-element.37.refs_0_), channel_id=1, source_target_pairs={{0,2},{1,3},{2,0},{3,1},{4,6},{5,7},{6,4},{7,5},{8,10},{9,11},{10,... | collective-permute-start | bytes 69896 | tf_op jit(solution)/shard_map/ppermute | solution.py:471
  11.7 3.4 %collective-permute-start.2 = (f32[8,728]{1,0:T(8,128)S(1)}, f32[8,728]{1,0:T(8,128)S(1)}, u32[]{:S(2)}, u32[]{:S(2)}) collective-permute-start(f32[8,728]{1,0:T(8,128)S(1)} %get-tuple-element.37.refs_0_), channel_id=1, source_target_pairs={{0,1},{1,0},{2,3},{3,2},{4,5},{5,4},{6,7},{7,6},{8,9},{9,8},{10,11... | collective-permute-start | bytes 69896 | tf_op jit(solution)/shard_map/ppermute | solution.py:471
  11.8 4.6 %collective-permute-start.6 = (bf16[384,768]{1,0:T(8,128)(2,1)S(1)}, bf16[384,768]{1,0:T(8,128)(2,1)S(1)}, u32[]{:S(2)}, u32[]{:S(2)}) collective-permute-start(bf16[384,768]{1,0:T(8,128)(2,1)S(1)} %get-tuple-element.39.depth_ref), channel_id=1, source_target_pairs={{0,1},{1,0},{2,3},{3,2},{4,5},{5,4},{6,7},{7,6},{8,9},{9,8},{10,11... | collective-permute-start | bytes 1769480 | tf_op jit(solution)/shard_map/ppermute | solution.py:467
  15.5 2.1 %collective-permute-start.5 = (bf16[384,768]{1,0:T(8,128)(2,1)S(1)}, bf16[384,768]{1,0:T(8,128)(2,1)S(1)}, u32[]{:S(2)}, u32[]{:S(2)}) collective-permute-start(bf16[384,768]{1,0:T(8,128)(2,1)S(1)} %get-tuple-element.41.full_ref), channel_id=1, source_target_pairs={{0,1},{1,0},{2,3},{3,2},{4,5},{5,4},{6,7},{7,6},{8,9},{9,8},{10,11... | collective-permute-start | bytes 1769480 | tf_op jit(solution)/shard_map/ppermute | solution.py:479
  18.6 9.1 %collective-permute-start.10 = (bf16[182,728]{1,0:T(8,128)(2,1)S(1)}, bf16[182,728]{1,0:T(8,128)(2,1)S(1)}, u32[]{:S(2)}, u32[]{:S(2)}) collective-permute-start(bf16[182,728]{1,0:T(8,128)(2,1)S(1)} %get-tuple-element.53), channel_id=1, source_target_pairs={{0,2},{1,3},{2,0},{3,1},{4,6},{5,7},{6,4},{7,5},{8,10},{9,11},{10,... | collective-permute-start | bytes 794984 | tf_op jit(solution)/shard_map/ppermute | solution.py:509
  19.1 5.6 %copy-start.3 = (f32[728]{0:T(1024)S(1)}, f32[728]{0:T(1024)}, u32[]{:S(2)}) copy-start(f32[728]{0:T(1024)} %shift_ref.1) | copy-start | bytes 8740
  21.6 1.3 %collective-permute-start.7 = (f32[16,728]{1,0:T(8,128)S(1)}, f32[16,728]{1,0:T(8,128)S(1)}, u32[]{:S(2)}, u32[]{:S(2)}) collective-permute-start(f32[16,728]{1,0:T(8,128)S(1)} %get-tuple-element.43.taps_ref), channel_id=1, source_target_pairs={{0,1},{1,0},{2,3},{3,2},{4,5},{5,4},{6,7},{7,6},{8,9},{9,8},{10,11... | collective-permute-start | bytes 139784 | tf_op jit(solution)/shard_map/ppermute | solution.py:522
  23.0 4.7 %collective-permute-start.11 = (f32[3,728]{1,0:T(4,128)S(1)}, f32[3,728]{1,0:T(4,128)S(1)}, u32[]{:S(2)}, u32[]{:S(2)}) collective-permute-start(f32[3,728]{1,0:T(4,128)S(1)} %get-tuple-element.55), channel_id=1, source_target_pairs={{0,2},{1,3},{2,0},{3,1},{4,6},{5,7},{6,4},{7,5},{8,10},{9,11},{10,... | collective-permute-start | bytes 26216 | tf_op jit(solution)/shard_map/ppermute | solution.py:526
  44.1 12.0 %all-to-all-start.1 = ((bf16[8,24,728]{2,1,0:T(8,128)(2,1)}), bf16[8,24,728]{2,1,0:T(8,128)(2,1)S(1)}, u32[]{:S(2)}, u32[]{:S(2)}) async-start(bf16[8,24,728]{2,1,0:T(8,128)(2,1)} %shard_map.137), calls=%async_computation.1 | async-start | bytes 589824 | tf_op jit(solution)/shard_map/all_to_all | solution.py:547
  47.5 1.3 %collective-permute-start.8 = (bf16[48,728]{1,0:T(8,128)(2,1)S(1)}, bf16[48,728]{1,0:T(8,128)(2,1)S(1)}, u32[]{:S(2)}, u32[]{:S(2)}) collective-permute-start(bf16[48,728]{1,0:T(8,128)(2,1)S(1)} %get-tuple-element.50), channel_id=1, source_target_pairs={{0,1},{1,0},{2,3},{3,2},{4,5},{5,4},{6,7},{7,6},{8,9},{9,8},{10,11... | collective-permute-start | bytes 209672 | tf_op jit(solution)/shard_map/ppermute | solution.py:548
  47.6 4.1 %collective-permute-start.9 = (bf16[48,728]{1,0:T(8,128)(2,1)S(1)}, bf16[48,728]{1,0:T(8,128)(2,1)S(1)}, u32[]{:S(2)}, u32[]{:S(2)}) collective-permute-start(bf16[48,728]{1,0:T(8,128)(2,1)S(1)} %get-tuple-element.51), channel_id=1, source_target_pairs={{0,3},{1,2},{2,1},{3,0},{4,7},{5,6},{6,5},{7,4},{8,11},{9,10},{10,... | collective-permute-start | bytes 209672 | tf_op jit(solution)/shard_map/ppermute | solution.py:549
